TPU v7x, 256 devices: a whole 4x4x8 slice. The times are simulated.
256 devices in a mesh: dp: 8 (over y, core), seq: 32 (over z, x).
Axes of the slice: x: 4, y: 4, z: 8, core: 2. Of those that a mesh axis runs over, the one named last changes fastest.
Arguments:
- point_rows: float32 [262144, 512], P(('dp', 'seq')), may hold values from -6 to 6
- serial_order: int32 [8, 32768], P('dp', 'seq'), may hold values from 0 to 32767, as said below
- scene_counts: int32 [8, 64], P('dp'), may hold values from 1 to 1024, 32768 in all within a row
- pool_counts: int32 [8, 32, 512], P('dp', 'seq'), may hold values from 1 to 3, 1024 in all within a row
- conv_gain: float32 [512], replicated, may hold values from 0.5 to 1.5
- conv_kernel: float32 [7, 512], replicated, may hold values from -2.5 to 2.5
- mixer_gain: float32 [512], replicated, may hold values from 0.5 to 1.5
- weight_in: bfloat16 [512, 2048], replicated, may hold values from -0.25 to 0.25
- weight_out: bfloat16 [2048, 512], replicated, may hold values from -0.125 to 0.125
- grad_out: float32 [131072, 512], P(('dp', 'seq')), may hold values from -6 to 6
Outputs:
- mixed_rows: float32 [131072, 512], P(('dp', 'seq'))
- grad_rows: float32 [262144, 512], P(('dp', 'seq'))
- grad_weight_in: float32 [512, 2048], P(None, 'seq')
- grad_weight_out: float32 [2048, 512], P('seq')
- grad_kernel: float32 [7, 512], replicated
- grad_conv_gain: float32 [512], replicated
- grad_mixer_gain: float32 [512], replicated
Inputs may be any that keep to these rules, and one draw needn't show every extreme that they name: `serial_order`: each row is a permutation of the group's rows. The 1024 serialized positions of one device take at most 48 rows from any one device's block of 1024 rows, and exactly 48 from some device.
All inputs are finite; a program needn't handle non-finite values.
Results may differ from a plain program's by a relative error of at most 0.0055.
Values sent between devices are 32-bit elements; how exact they have to be, the bound alone decides.
A program may use at most 128 MiB of HBM per device.

v0:
```python
import jax
import jax.numpy as jnp
from jax import lax
from jax.sharding import PartitionSpec as P

NORM_EPS = 1e-05


def padded_2(shard, sides, width):
    for axis, dim in sides:
        count, length = (lax.axis_size(axis), shard.shape[dim])
        up = [(i, (i + 1) % count) for i in range(count - 1)]
        down = [(j, i) for i, j in up]
        last = lax.slice_in_dim(shard, length - width, length, axis=dim)
        initial = lax.slice_in_dim(shard, 0, width, axis=dim)
        before = lax.ppermute(last, axis, up)
        after = lax.ppermute(initial, axis, down)
        shard = jnp.concatenate([before, shard, after], axis=dim)
    return shard


def layer_norm(values, gain_vec):
    centre = values - jnp.mean(values, axis=-1, keepdims=True)
    spread = jnp.mean(centre * centre, axis=-1, keepdims=True)
    return centre * lax.rsqrt(spread + NORM_EPS) * gain_vec


def mixer_forward(pooled, gain_vec, weight_in, weight_out):
    normed = layer_norm(pooled, gain_vec).astype(jnp.bfloat16)
    hidden = jnp.dot(normed, weight_in, preferred_element_type=jnp.float32)
    active = jax.nn.gelu(hidden).astype(jnp.bfloat16)
    mixed_rows = pooled + jnp.dot(active, weight_out, preferred_element_type=jnp.float32)
    return (normed, hidden, active, mixed_rows)


def mixer_backward(pooled, gain_vec, weight_in, weight_out, normed, hidden, active, grad_mixed):
    grad_low = grad_mixed.astype(jnp.bfloat16)
    first_dims = (((0,), (0,)), ((), ()))
    last_dims = (((1,), (1,)), ((), ()))
    grad_wout = lax.dot_general(active, grad_low, first_dims, preferred_element_type=jnp.float32)
    grad_active = lax.dot_general(
        grad_low, weight_out, last_dims, preferred_element_type=jnp.float32
    )
    grad_hidden = jax.vjp(jax.nn.gelu, hidden)[1](grad_active)[0].astype(jnp.bfloat16)
    grad_win = lax.dot_general(normed, grad_hidden, first_dims, preferred_element_type=jnp.float32)
    grad_normed = lax.dot_general(
        grad_hidden, weight_in, last_dims, preferred_element_type=jnp.float32
    )
    back_fn = jax.vjp(layer_norm, pooled, gain_vec)[1]
    grad_ln_in, grad_gain = back_fn(grad_normed)
    return (grad_mixed + grad_ln_in, grad_gain, grad_win, grad_wout)


def compact(chosen, values, capacity):
    order_rank = jnp.cumsum(chosen.astype(jnp.int32), axis=1) - 1
    slot_ids = jnp.arange(capacity, dtype=jnp.int32)
    matched = chosen[:, None, :] & (order_rank[:, None, :] == slot_ids[None, :, None])
    picked = jnp.sum(jnp.where(matched, values[:, None, :], 0), axis=2)
    filled = jnp.any(matched, axis=2)
    return (picked, filled)


def body(
    point_rows,
    serial_order,
    scene_counts,
    pool_counts,
    conv_gain,
    conv_kernel,
    mixer_gain,
    weight_in,
    weight_out,
    grad_out,
):
    seq_count = lax.axis_size("seq")
    myself = lax.axis_index("seq")
    row_count = point_rows.shape[0]
    channels = point_rows.shape[1]
    taps = conv_kernel.shape[0]
    half_width = taps // 2
    capacity = 3 * (row_count // (2 * seq_count))
    own_order = serial_order[0]
    owner_dev = own_order // row_count
    peer_ids = jnp.arange(seq_count, dtype=jnp.int32)
    from_peer = owner_dev[None, :] == peer_ids[:, None]
    positions = jnp.arange(row_count, dtype=jnp.int32)
    slot_pos, slot_used = compact(from_peer, positions[None, :], capacity)
    every_order = lax.all_gather(serial_order, "seq", axis=1, tiled=True).reshape(
        seq_count, row_count
    )
    wanted = every_order // row_count == myself
    send_index, send_used = compact(wanted, every_order % row_count, capacity)
    outgoing = point_rows[send_index.reshape(-1)].reshape(seq_count, capacity, channels)
    incoming = lax.all_to_all(outgoing, "seq", split_axis=0, concat_axis=0, tiled=True)
    target = jnp.where(slot_used, slot_pos, row_count).reshape(-1)
    serial = (
        jnp.zeros((row_count, channels), jnp.float32)
        .at[target]
        .set(incoming.reshape(-1, channels), mode="drop")
    )
    scene_ends = jnp.cumsum(scene_counts[0])
    global_pos = myself * row_count + jnp.arange(
        -half_width, row_count + half_width, dtype=jnp.int32
    )
    scene_ids = jnp.sum((global_pos[:, None] >= scene_ends[None, :]).astype(jnp.int32), axis=1)
    inside_group = (global_pos >= 0) & (global_pos < seq_count * row_count)
    scene_ids = jnp.where(inside_group, scene_ids, -1)
    centre_ids = scene_ids[half_width : half_width + row_count]
    padded = padded_2(serial, (("seq", 0),), half_width)
    normed_pad = layer_norm(padded, conv_gain)
    conved = serial
    for offset in range(taps):
        same_scene = (scene_ids[offset : offset + row_count] == centre_ids).astype(jnp.float32)
        conved = (
            conved
            + conv_kernel[offset] * same_scene[:, None] * normed_pad[offset : offset + row_count]
        )
    pool_len = pool_counts[0, 0]
    pool_ends = jnp.cumsum(pool_len)
    pool_starts = pool_ends - pool_len
    pool_ids = jnp.sum((positions[:, None] >= pool_ends[None, :]).astype(jnp.int32), axis=1)
    lengths = pool_len.astype(jnp.float32)[:, None]
    summed = jnp.zeros((pool_len.shape[0], channels), jnp.float32)
    for member_idx in range(3):
        member_row = jnp.minimum(pool_starts + member_idx, row_count - 1)
        taken = (member_idx < pool_len)[:, None]
        summed = summed + jnp.where(taken, conved[member_row], 0.0)
    pooled = summed / lengths
    normed, hidden, active, mixed_rows = mixer_forward(pooled, mixer_gain, weight_in, weight_out)
    grad_pooled, grad_mgain, grad_win, grad_wout = mixer_backward(
        pooled, mixer_gain, weight_in, weight_out, normed, hidden, active, grad_out
    )
    grad_conved = (grad_pooled / lengths)[pool_ids]
    grad_padded = padded_2(grad_conved, (("seq", 0),), half_width)
    grad_lnorm = jnp.zeros_like(serial)
    kernel_terms = []
    for offset in range(taps):
        same_scene = (scene_ids[offset : offset + row_count] == centre_ids).astype(jnp.float32)
        kernel_terms.append(
            jnp.sum(
                same_scene[:, None] * normed_pad[offset : offset + row_count] * grad_conved, axis=0
            )
        )
        back_pos = 2 * half_width - offset
        same_back = (scene_ids[back_pos : back_pos + row_count] == centre_ids).astype(jnp.float32)
        grad_lnorm = (
            grad_lnorm
            + conv_kernel[offset]
            * same_back[:, None]
            * grad_padded[back_pos : back_pos + row_count]
        )
    grad_kern = jnp.stack(kernel_terms)
    back_fn = jax.vjp(layer_norm, serial, conv_gain)[1]
    grad_ln_in, grad_cgain = back_fn(grad_lnorm)
    grad_serial = grad_conved + grad_ln_in
    back_rows = grad_serial[jnp.where(slot_used, slot_pos, 0).reshape(-1)].reshape(
        seq_count, capacity, channels
    )
    returned = lax.all_to_all(back_rows, "seq", split_axis=0, concat_axis=0, tiled=True)
    target_back = jnp.where(send_used, send_index, row_count).reshape(-1)
    grad_rows = (
        jnp.zeros_like(point_rows).at[target_back].set(returned.reshape(-1, channels), mode="drop")
    )
    grad_kern, grad_cgain, grad_mgain = lax.psum((grad_kern, grad_cgain, grad_mgain), ("dp", "seq"))
    part_in, part_out = (
        lax.psum_scatter(grad_win, "seq", scatter_dimension=1, tiled=True),
        lax.psum_scatter(grad_wout, "seq", scatter_dimension=0, tiled=True),
    )
    grad_win, grad_wout = lax.psum((part_in, part_out), "dp")
    return (mixed_rows, grad_rows, grad_win, grad_wout, grad_kern, grad_cgain, grad_mgain)


def solution(mesh):
    return jax.shard_map(
        body,
        mesh=mesh,
        in_specs=(
            P(("dp", "seq"), None),
            P("dp", "seq"),
            P("dp", None),
            P("dp", "seq", None),
            P(),
            P(),
            P(),
            P(),
            P(),
            P(("dp", "seq"), None),
        ),
        out_specs=(
            P(("dp", "seq"), None),
            P(("dp", "seq"), None),
            P(None, "seq"),
            P("seq", None),
            P(),
            P(),
            P(),
        ),
        check_vma=False,
    )
```

profile of v0, /device:TPU:1, one launch (start us, length us, event | category | flops | bytes accessed | tf_op | source)
XLA Modules:
  0.0 774.5 jit_solution(15451745387094078613)
XLA Ops:
  7.2 37.2 %all_gather.3 = s32[1,32768]{1,0:T(1,128)S(1)} all-gather(s32[1,1024]{1,0:T(1,128)} %param.11), channel_id=1, replica_groups=mesh['dp'=8,'seq'=32] {'seq'}, dimensions={1}, use_global_device_ids=true | all-gather | bytes 135168 | tf_op jit(solution)/shard_map/all_gather | solution.py:88
  44.4 0.5 broadcast.617
  44.9 0.9 reduce.20
  46.1 9.0 %reduce-window.34 = s32[32,8,128]{2,1,0:T(8,128)S(1)} reduce-window(s32[32,8,128]{2,1,0:T(8,128)S(1)} %fusion.38, s32[]{:T(128)} %constant.90.clone.1), window={size=1x1x128 pad=0_0x0_0x127_0}, to_apply=%region_4.5 | reduce-window | flops 4161536 | bytes 262148 | tf_op jit(solution)/shard_map/reduce-window.2
  55.2 0.1 copy.29
  55.6 1.2 fusion.3
  56.9 1.7 select_reduce_fusion
  58.8 7.3 gather_fusion
  66.2 6.4 all-to-all-start
  72.6 0.2 reduce-scatter.5.cloned.1.call-start
  72.8 0.3 reduce-window.44
  73.6 9.0 %reduce-window.30 = s32[32,8,128]{2,1,0:T(8,128)S(1)} reduce-window(s32[32,8,128]{2,1,0:T(8,128)S(1)} %fusion.35, s32[]{:T(128)} %constant.90.clone.1), window={size=1x1x128 pad=0_0x0_0x127_0}, to_apply=%region_0.1 | reduce-window | flops 4161536 | bytes 262148 | tf_op jit(solution)/shard_map/reduce-window
  82.7 0.1 copy.27
  83.1 1.2 fusion.1
  84.4 1.8 select_reduce_fusion.1
  86.2 0.1 slice_reduce_fusion
  86.8 48.7 %all-to-all-done = f32[32,48,512]{2,1,0:T(8,128)} async-done(((f32[32,48,512]{2,1,0:T(8,128)}), f32[32,48,512]{2,1,0:T(8,128)}, u32[]{:S(2)}, u32[]{:S(2)}) %all-to-all-start) | async-done | bytes 3145760 | tf_op jit(solution)/shard_map/all_to_all | solution.py:94
  135.4 9.0 %scatter_custom_fusion = f32[1024,512]{1,0:T(8,128)} fusion(s32[1536]{0:T(1024)S(1)} %fusion.40, f32[1536,512]{1,0:T(8,128)} %bitcast.6, f32[]{:T(128)} %constant.91.clone.1), kind=kCustom, calls=%fused_computation.70 | custom fusion | bytes 2097664 | tf_op jit(solution)/shard_map/scatter | solution.py:99
  144.4 0.7 fusion.59
  145.1 1.3 collective-permute-start.1
  146.4 4.2 collective-permute-start
  150.7 0.5 collective-permute-done
  151.2 8.2 %concatenate.14 = f32[1030,512]{1,0:T(8,128)} concatenate(f32[3,512]{1,0:T(4,128)S(1)} %collective-permute-done, f32[1024,512]{1,0:T(8,128)} %scatter_custom_fusion, f32[3,512]{1,0:T(4,128)S(1)} %collective-permute-done.1), dimensions={0} | concatenate | bytes 4218880 | tf_op jit(solution)/shard_map/concatenate | solution.py:18
  159.4 1.9 reduce_sum.210
  161.2 2.2 multiply_reduce_fusion
  163.4 0.3 multiply_multiply_fusion.2
  163.8 1.9 copy-done.4
  165.7 3.5 multiply_add_fusion
  169.2 4.3 gather_fusion.3
  173.5 4.3 gather_fusion.2
  177.9 4.3 gather_fusion.1
  182.2 2.3 fusion.57
  184.5 0.3 multiply_reduce_fusion.13
  184.8 1.3 fusion.53
  186.1 1.9 copy-done.8
  188.0 3.8 fusion.26
  191.9 0.3 reduce-scatter.3.cloned.1.call-start
  192.4 0.3 convert_reduce_fusion
  192.7 1.8 reduce_sum.252
  194.6 2.1 multiply_reduce_fusion.10
  196.7 5.7 fusion.10
  202.4 1.5 multiply_reduce_fusion.11
  203.9 0.4 fusion.56
  204.4 0.2 add_divide_fusion
  204.6 4.9 gather_fusion.4
  209.5 5.0 fusion.52
  214.5 0.7 fusion.58
  215.3 1.6 collective-permute-start.2
  216.8 1.8 constant_dynamic-update-slice_fusion.1
  218.6 4.2 collective-permute-start.3
  222.9 0.8 collective-permute-done.3
  223.6 3.6 multiply_reduce_fusion.1
  227.3 0.8 fusion.54
  228.1 0.7 copy-done.3
  228.9 2.8 multiply_reduce_fusion.2
  231.6 5.0 gather_fusion.5
  236.6 12.4 %all-to-all-start.1 = ((f32[32,48,512]{2,1,0:T(8,128)}), f32[32,48,512]{2,1,0:T(8,128)}, u32[]{:S(2)}, u32[]{:S(2)}) async-start(f32[32,48,512]{2,1,0:T(8,128)} %bitcast.59), calls=%async_computation.1 | async-start | bytes 6291456 | tf_op jit(solution)/shard_map/all_to_all | solution.py:159
  249.0 197.9 %reduce-scatter.5.cloned.1.call-done = f32[64,512]{1,0:T(8,128)} async-done(((f32[2048,512]{1,0:T(8,128)}), f32[64,512]{1,0:T(8,128)}) %reduce-scatter.5.cloned.1.call-update) | async-done | bytes 131088 | tf_op jit(solution)/shard_map/reduce_scatter | solution.py:167
  446.9 223.7 %reduce-scatter.3.cloned.1.call-done = f32[512,64]{0,1:T(8,128)} async-done(((f32[512,2048]{0,1:T(8,128)}), f32[512,64]{0,1:T(8,128)}) %reduce-scatter.3.cloned.1.call-update) | async-done | bytes 131088 | tf_op jit(solution)/shard_map/reduce_scatter | solution.py:166
  670.6 5.4 convolution_add_fusion
  676.1 79.7 %all-reduce = (f32[7,512]{1,0:T(8,128)}, f32[512]{0:T(512)}, f32[512]{0:T(512)}) all-reduce(f32[7,512]{1,0:T(8,128)S(1)} %stack.31, f32[512]{0:T(512)S(1)} %get-tuple-element.14, f32[512]{0:T(512)S(1)} %get-tuple-element.16), channel_id=1, replica_groups=mesh['dp'=8,'seq'=32] {'dp','seq'}, use_global_device_ids=true, to_apply=%region_36.37 | all-reduce | flops 4608 | bytes 36864 | tf_op jit(solution)/shard_map/psum | solution.py:164
  755.9 9.0 %scatter_custom_fusion.1 = f32[1024,512]{1,0:T(8,128)} fusion(s32[1536]{0:T(1024)S(1)} %get-tuple-element.18, f32[1536,512]{1,0:T(8,128)} %bitcast.26, f32[]{:T(128)} %constant.91.clone.1), kind=kCustom, calls=%fused_computation.68 | custom fusion | bytes 2097664 | tf_op jit(solution)/shard_map/scatter | solution.py:162
  764.8 1.6 copy.44
  766.4 1.6 copy.45
  (101 shorter events, 2.6 us)
Async XLA Ops:
  7.2 177.6 %copy-start = (bf16[512,2048]{1,0:T(8,128)(2,1)S(1)}, bf16[512,2048]{1,0:T(8,128)(2,1)}, u32[]{:S(2)}) copy-start(bf16[512,2048]{1,0:T(8,128)(2,1)} %param.17) | copy-start | bytes 6291460
  66.2 6.6 copy-start.13
  66.2 7.1 copy-start.17
  66.2 7.4 copy-start.15
  66.2 69.3 %all-to-all-start = ((f32[32,48,512]{2,1,0:T(8,128)}), f32[32,48,512]{2,1,0:T(8,128)}, u32[]{:S(2)}, u32[]{:S(2)}) async-start(f32[32,48,512]{2,1,0:T(8,128)} %bitcast.58), calls=%async_computation | async-start | bytes 6291456 | tf_op jit(solution)/shard_map/all_to_all | solution.py:94
  72.6 14.2 %copy-start.16 = (f32[7,512]{1,0:T(8,128)S(1)}, f32[7,512]{1,0:T(8,128)}, u32[]{:S(2)}) copy-start(f32[7,512]{1,0:T(8,128)} %param.15) | copy-start | bytes 43012
  72.6 374.4 %reduce-scatter.5.cloned.1.call-start = ((), (), s32[]{:S(2)}) async-start(), calls=%async_computation.5 | async-start | bytes 4325376 | tf_op jit(solution)/shard_map/reduce_scatter | solution.py:167
  145.1 5.5 collective-permute-start.1
  146.4 4.8 collective-permute-start
  159.4 4.0 copy-start.14
  161.2 2.2 copy-start.6
  163.4 2.2 copy-start.4
  163.8 5.4 copy-start.2
  182.2 2.6 copy-start.12
  184.8 3.2 copy-start.10
  186.1 1.9 copy-start.8
  191.9 478.7 %reduce-scatter.3.cloned.1.call-start = ((), (), s32[]{:S(2)}) async-start(), calls=%async_computation.4 | async-start | bytes 4325376 | tf_op jit(solution)/shard_map/reduce_scatter | solution.py:166
  194.5 2.1 copy-start.11
  202.4 1.5 copy-start.9
  215.3 8.4 %copy-start.5 = (f32[1024,512]{1,0:T(8,128)S(1)}, f32[1024,512]{1,0:T(8,128)}, u32[]{:S(2)}) copy-start(f32[1024,512]{1,0:T(8,128)} %scatter_custom_fusion) | copy-start | bytes 6291460
  215.3 8.4 %copy-start.7 = (f32[1024,512]{1,0:T(8,128)S(1)}, f32[1024,512]{1,0:T(8,128)}, u32[]{:S(2)}) copy-start(f32[1024,512]{1,0:T(8,128)} %gather_fusion.4) | copy-start | bytes 6291460
  215.3 7.6 collective-permute-start.2
  218.6 5.0 collective-permute-start.3
  227.3 1.6 copy-start.3
  236.6 519.3 %all-to-all-start.1 = ((f32[32,48,512]{2,1,0:T(8,128)}), f32[32,48,512]{2,1,0:T(8,128)}, u32[]{:S(2)}, u32[]{:S(2)}) async-start(f32[32,48,512]{2,1,0:T(8,128)} %bitcast.59), calls=%async_computation.1 | async-start | bytes 6291456 | tf_op jit(solution)/shard_map/all_to_all | solution.py:159
  249.0 515.8 %all-reduce.4.cloned.1.call-start = ((), (), s32[]{:S(2)}) async-start(), calls=%async_computation.6 | async-start | bytes 524288 | tf_op jit(solution)/shard_map/psum | solution.py:169
  670.6 97.3 %copy-start.1 = (bf16[512,2048]{1,0:T(8,128)(2,1)S(1)}, bf16[512,2048]{1,0:T(8,128)(2,1)}, u32[]{:S(2)}) copy-start(bf16[512,2048]{1,0:T(8,128)(2,1)} %param.17) | copy-start | bytes 6291460
Sparse Core Ops, SparseCore 0:
  192.0 254.8 reduce-scatter.4
  451.3 219.2 reduce-scatter.2
  673.0 66.0 all-reduce.3
where the time goes:
time: 776 us; the launch traced here: 774 us
  waiting for transfers between devices  472 us (61%)
  blocking collectives  117 us (15%)
  local copies, waits for them, and re-layouts  69.1 us (9%)
  other arithmetic  49.1 us (6%)
  starting transfers between devices  30.6 us (4%)
  matrix products  22.8 us (3%)
  between operations  14.4 us (2%)
    reduce_scatter x1, waiting for transfers between devices, body(): lax.psum_scatter(grad_win, 'seq', scatter_dimension=1, tiled=True)  224 us
    reduce_scatter x1, waiting for transfers between devices, body(): lax.psum_scatter(grad_wout, 'seq', scatter_dimension=0, tiled=True)  198 us
    psum x1, blocking collectives, body(): lax.psum((grad_kern, grad_cgain, grad_mgain), ('dp', 'seq'))  79.7 us
    all_to_all x1, waiting for transfers between devices, body(): lax.all_to_all(outgoing, 'seq', split_axis=0, concat_axis=0, tiled=True)  48.7 us
    all_gather x1, blocking collectives, body(): lax.all_gather(serial_order, 'seq', axis=1, tiled=True)  37.2 us
    another operation x10, other arithmetic  18.8 us
  transfers between devices with their start and end apart: 9, of which 5 were waited for; matrix products, arithmetic and copies ran while one was open for 8% of the time, Pallas kernels for 0%

commit v1 on v0

v1 whole, which is shorter than its diff:
```python
import jax
import jax.numpy as jnp
from jax import lax
from jax.experimental import pallas as pl
from jax.experimental.pallas import tpu as pltpu
from jax.sharding import PartitionSpec as P

NORM_EPS = 1e-05
MESH = pl.DeviceIdType.MESH
f32, bf16 = jnp.float32, jnp.bfloat16
NX = 4
CH = 32
PAD = 8
GELU_A = 0.7978845608028654
GELU_B = 0.044715


def iota_f(shape, dim):
    return lax.broadcasted_iota(jnp.int32, shape, dim).astype(f32)


def ones_where(mask):
    return jnp.where(mask, 1.0, 0.0)


def split_hi_lo(value):
    high = value.astype(bf16)
    return high, (value - high.astype(f32)).astype(bf16)


def mm(a, b):
    return jnp.dot(a, b, preferred_element_type=f32)


def mm_last(a, b):
    return lax.dot_general(a, b, (((1,), (1,)), ((), ())), preferred_element_type=f32)


def mm_first(a, b):
    return lax.dot_general(a, b, (((0,), (0,)), ((), ())), preferred_element_type=f32)


def fold8(value):
    return jnp.sum(value.reshape(value.shape[0] // 8, 8, value.shape[1]), axis=0)


def rows_from(window, offset, count):
    size = window.shape[0]
    return pltpu.roll(window, (size - offset) % size, 0)[0:count]


def wide(value):
    return jnp.concatenate([value] * 4, axis=1)


def kernel(
    n_dp, n_seq, cap,
    rows_hbm, order_ref, scene_ref, pool_ref, cgain_ref, taps_ref, mgain_ref, win_hbm, wout_hbm, gout_hbm,
    mixed_hbm, grows_hbm, gwin_ref, gwout_ref, gtaps_ref, gcg_ref, gmg_ref,
    rows_v, rows_hi, rows_lo, list_s, list_r, kmat, scol, srow, tcol, pick,
    outb, inb, inb2, ser, xhat, rstd, sid, val_hi, val_lo,
    pool_m, pool_t, plen, gout_v, glow, mixed_v, xhat2, norm2, gnorm, rstd2,
    win_v, wout_v, gw, rc, ry, wx, rx, wz, rz, fin, gc, gtap_acc, small, rs1, rs2, rs3,
    ld_sem, idx_s, idx_r, row_s, row_r, back_s, back_r, halo_s, halo_r,
    core_s, core_r, y_s, y_r, x_s, x_r, z_s, z_r, s1_s, s1_r, s2_s, s2_r, s3_s, s3_r, f_s, f_r,
):
    count, chans = rows_v.shape
    segs = mixed_v.shape[0]
    hidden = wout_v.shape[0]
    n_y, n_z = n_dp // 2, n_seq // NX
    group = 8
    n_groups = n_seq // group
    slots = group * cap
    dp, me = lax.axis_index("dp"), lax.axis_index("seq")
    y, core = lax.div(dp, 2), lax.rem(dp, 2)
    z, x = lax.div(me, NX), lax.rem(me, NX)
    my_group = lax.div(me, group)

    def remote(src, dst, send, recv, to_dp, to_seq):
        return pltpu.make_async_remote_copy(
            src_ref=src, dst_ref=dst, send_sem=send, recv_sem=recv,
            device_id=(to_dp, to_seq), device_id_type=MESH,
        )

    def each(n, fn, start=0):
        def step(i, carry):
            fn(i)
            return carry
        lax.fori_loop(start, n, step, 0)

    loads = [
        pltpu.make_async_copy(rows_hbm, rows_v, ld_sem.at[0]),
        pltpu.make_async_copy(win_hbm, win_v, ld_sem.at[1]),
        pltpu.make_async_copy(wout_hbm, wout_v, ld_sem.at[2]),
        pltpu.make_async_copy(gout_hbm, gout_v, ld_sem.at[3]),
    ]
    for load in loads:
        load.start()

    barrier = pltpu.get_barrier_semaphore()
    each(n_seq, lambda i: pl.semaphore_signal(
        barrier, inc=1, device_id=(dp, lax.rem(me + i, n_seq)), device_id_type=MESH), 1)
    each(n_dp, lambda i: pl.semaphore_signal(
        barrier, inc=1, device_id=(lax.rem(dp + i, n_dp), me), device_id_type=MESH), 1)

    order = order_ref[...]
    shift = count.bit_length() - 1
    owner = (order >> shift).astype(f32)
    local = order & (count - 1)
    local_hi = (local >> 5).astype(f32)
    local_lo = (local & 31).astype(f32)
    owner_col = jnp.transpose(jnp.broadcast_to(owner, (128, count)))
    lane = iota_f((128, 128), 1)
    below = ones_where(iota_f((128, 128), 0) > lane).astype(bf16)
    before = jnp.zeros((1, 128), f32)
    for b in range(count // 128):
        own_b = owner_col[b * 128:(b + 1) * 128]
        hot = ones_where(own_b == lane)
        ranks = mm(below, hot.astype(bf16)) + before
        before = before + jnp.sum(hot, axis=0, keepdims=True)
        rank = jnp.broadcast_to(jnp.sum(hot * ranks, axis=1, keepdims=True), (128, 128))
        scol[b * 128:(b + 1) * 128, :] = own_b * cap + rank
        kmat[b * 128:(b + 1) * 128, :] = ones_where(rank == lane).astype(bf16)
    srow[...] = jnp.transpose(scol[...])[0:8, :]
    owner_hot = ones_where(jnp.broadcast_to(owner, (n_seq, count)) == iota_f((n_seq, count), 0))
    kval = kmat[...]
    lists = (
        mm((owner_hot * local_hi).astype(bf16), kval) * 32.0
        + mm((owner_hot * local_lo).astype(bf16), kval)
        + mm(owner_hot.astype(bf16), kval)
        - 1.0
    )
    for p in range(n_seq):
        list_s[p] = jnp.broadcast_to(lists[p:p + 1, :], (8, 128))
    list_r[me] = list_s[me]

    pl.semaphore_wait(barrier, n_seq - 1 + n_dp - 1)

    def send_list(i):
        p = lax.rem(me + i, n_seq)
        return remote(list_s.at[p], list_r.at[me], idx_s.at[p], idx_r.at[me], dp, p)

    def recv_list(i):
        p = lax.rem(me + i, n_seq)
        return remote(list_s.at[p], list_r.at[p], idx_s.at[p], idx_r.at[p], dp, p)

    each(n_seq, lambda i: send_list(i).start(), 1)

    loads[0].wait()

    def split_rows(i):
        at = pl.ds(pl.multiple_of(i * CH, CH), CH)
        rows_hi[at, :], rows_lo[at, :] = split_hi_lo(rows_v[at, :])

    each(count // CH, split_rows)
    each(n_seq, lambda i: recv_list(i).wait_recv(), 1)

    tcol[...] = jnp.transpose(list_r[...].reshape(n_seq * 8, 128))

    def row_out(p, src, dst, send, recv):
        return remote(src.at[p], dst.at[me], send.at[p], recv.at[me], dp, p)

    def row_self(src, dst, recv):
        return pltpu.make_async_copy(src.at[me], dst.at[me], recv.at[me])

    def launch(p0, dst, send, recv):
        def one(i):
            p = p0 + i

            @pl.when(p != me)
            def _():
                row_out(p, outb, dst, send, recv).start()

            @pl.when(p == me)
            def _():
                row_self(outb, dst, recv).start()
        each(group, one)

    def arrive(p0, dst, send, recv):
        def one(i):
            p = p0 + i

            @pl.when(p != me)
            def _():
                remote(outb.at[p], dst.at[p], send.at[p], recv.at[p], dp, p).wait_recv()

            @pl.when(p == me)
            def _():
                row_self(outb, dst, recv).wait()
        each(group, one)

    def group_out(g):
        return group * lax.rem(my_group + g, n_groups)

    def group_in(g):
        return group * lax.rem(my_group + n_groups - g, n_groups)

    tlane = lax.broadcasted_iota(jnp.int32, (cap, n_seq * 8), 1)
    rlane = iota_f((cap, count), 1)

    def gather_group(g):
        p0 = group_out(g)

        def one(i):
            p = p0 + i
            col = jnp.sum(jnp.where(tlane == p * 8, tcol[0:cap, :], 0.0), axis=1, keepdims=True)
            pick[pl.ds(pl.multiple_of(p * cap, 16), cap), :] = ones_where(
                jnp.broadcast_to(col, (cap, count)) == rlane).astype(bf16)
        each(group, one)
        hot = pick[pl.ds(pl.multiple_of(p0 * cap, 16), slots), :]
        made = mm(hot, rows_hi[...]) + mm(hot, rows_lo[...])
        outb[pl.ds(p0, group)] = made.reshape(group, cap, chans)
        launch(p0, inb, row_s, row_r)

    each(n_groups, gather_group)

    scene_n = scene_ref.shape[1]
    upto = ones_where(iota_f((scene_n, scene_n), 0) <= iota_f((scene_n, scene_n), 1))
    scene_ends = lax.dot_general(
        jnp.broadcast_to(scene_ref[...].astype(f32), (8, scene_n)), upto, (((1,), (0,)), ((), ())),
        precision=lax.Precision.HIGHEST, preferred_element_type=f32)[0:1, :]
    first_pos = (me * count - PAD).astype(f32)

    def scenes(i):
        start = pl.multiple_of(i * 8, 8)
        pos = iota_f((8, scene_n), 0) + (first_pos + start.astype(f32))
        ids = jnp.sum(ones_where(pos >= scene_ends), axis=1, keepdims=True)
        ids = jnp.where(pos[:, 0:1] < 0.0, -1.0, ids)
        sid[pl.ds(start, 8), :] = jnp.broadcast_to(ids, (8, 128))

    each(sid.shape[0] // 8, scenes)

    lens = jnp.broadcast_to(pool_ref[...].astype(f32), (128, segs))
    len_col = jnp.transpose(lens)
    plen[...] = len_col
    tri_rows, tri_cols = iota_f((segs, segs), 0), iota_f((segs, segs), 1)
    end_col = mm(ones_where(tri_cols <= tri_rows).astype(bf16), len_col.astype(bf16))
    end_row = mm(lens[0:8].astype(bf16), ones_where(tri_rows <= tri_cols).astype(bf16))[0:1, :]
    start_col = end_col - len_col
    start_row = end_row - lens[0:1]
    for t in range(count // 128):
        at_pos = iota_f((segs, 128), 1) + float(t * 128)
        pool_m[:, t * 128:(t + 1) * 128] = ones_where((at_pos >= start_col) & (at_pos < end_col)).astype(bf16)

    def pool_rows(i):
        start = pl.multiple_of(i * CH, CH)
        at_pos = iota_f((CH, segs), 0) + start.astype(f32)
        pool_t[pl.ds(start, CH), :] = ones_where((at_pos >= start_row) & (at_pos < end_row)).astype(bf16)

    each(count // CH, pool_rows)

    def clear(i):
        ser[pl.ds(pl.multiple_of(i * 8 + PAD, 8), 8), :] = jnp.zeros((8, chans), f32)

    each(count // 8, clear)
    gtap_acc[...] = jnp.zeros(gtap_acc.shape, f32)

    slane = iota_f((count, 128), 1)

    def place_group(g):
        p0 = group_in(g)
        arrive(p0, inb, row_s, row_r)
        high, low = split_hi_lo(inb[pl.ds(p0, group)].reshape(slots, chans))
        at_slot = scol[...] - (p0 * cap).astype(f32)
        hot = jnp.concatenate(
            [ones_where(at_slot == slane + float(128 * t)).astype(bf16) for t in range(slots // 128)], axis=1)
        ser[pl.ds(PAD, count), :] += mm(hot, high) + mm(hot, low)

    each(n_groups, place_group)

    right, left = lax.rem(me + 1, n_seq), lax.rem(me + n_seq - 1, n_seq)

    def halo(buf, k):
        return (
            remote(buf.at[pl.ds(count, PAD)], buf.at[pl.ds(0, PAD)], halo_s.at[k], halo_r.at[k], dp, right),
            remote(buf.at[pl.ds(PAD, PAD)], buf.at[pl.ds(count + PAD, PAD)], halo_s.at[k + 1], halo_r.at[k + 1],
                   dp, left),
        )

    for copy in halo(ser, 0):
        copy.start()

    inv = 1.0 / chans

    def norm_rows(start, rows):
        at = pl.ds(start, rows)
        v = ser[at, :]
        centre = v - jnp.sum(v, axis=1, keepdims=True) * inv
        r = lax.rsqrt(jnp.sum(centre * centre, axis=1, keepdims=True) * inv + NORM_EPS)
        xhat[at, :] = centre * r
        rstd[at, :] = jnp.broadcast_to(r, (rows, 128))

    each(count // CH, lambda i: norm_rows(pl.multiple_of(i * CH + PAD, 8), CH))
    half = taps_ref.shape[0] // 2
    taps = taps_ref[...]
    cgain = cgain_ref[...]
    taps_gain = taps * cgain

    def conv_rows(i):
        base = pl.multiple_of(i * CH, CH)
        here = sid[pl.ds(base + PAD, CH), :]
        total = ser[pl.ds(base + PAD, CH), :]
        around = xhat[pl.ds(base, CH + 2 * PAD), :]
        for d in range(2 * half + 1):
            same = wide(ones_where(sid[pl.ds(base + PAD + d - half, CH), :] == here))
            total = total + taps_gain[d:d + 1, :] * (same * rows_from(around, PAD + d - half, CH))
        at = pl.ds(base, CH)
        val_hi[at, :], val_lo[at, :] = split_hi_lo(total)

    n_chunks = count // CH
    each(n_chunks - 1, conv_rows, 1)
    for copy in halo(ser, 0):
        copy.wait_recv()
    norm_rows(0, PAD)
    norm_rows(count + PAD, PAD)
    each(2, lambda i: conv_rows(i * (n_chunks - 1)))

    mixed_v[...] = mm(pool_m[...], val_hi[...]) + mm(pool_m[...], val_lo[...])
    mgain = mgain_ref[...]
    loads[3].wait()

    def norm_pooled(i):
        at = pl.ds(pl.multiple_of(i * CH, CH), CH)
        v = mixed_v[at, :] / wide(plen[at, :])
        centre = v - jnp.sum(v, axis=1, keepdims=True) * inv
        r = lax.rsqrt(jnp.sum(centre * centre, axis=1, keepdims=True) * inv + NORM_EPS)
        unit = centre * r
        mixed_v[at, :] = v
        xhat2[at, :] = unit
        norm2[at, :] = (unit * mgain).astype(bf16)
        rstd2[at, :] = jnp.broadcast_to(r, (CH, 128))
        glow[at, :] = gout_v[at, :].astype(bf16)
        gnorm[at, :] = jnp.zeros((CH, chans), f32)

    each(segs // CH, norm_pooled)
    loads[1].wait()
    loads[2].wait()

    hb = 512
    n_hb = hidden // hb
    n_cols = chans // 128
    partner = dp + 1 - 2 * core

    def core_copy(j):
        at = pl.ds(pl.multiple_of(j * hb, hb), hb)
        return remote(gw.at[1 - core, :, at, :], rc.at[:, at, :], core_s.at[j], core_r.at[j], partner, me)

    def mlp_block(j):
        at_h = pl.ds(pl.multiple_of(j * hb, hb), hb)
        w_in, w_out = win_v[:, at_h], wout_v[at_h, :]
        n2, gl = norm2[...], glow[...]
        rows_v[0:segs, :] = mm(n2, w_in)
        rows_v[segs:2 * segs, :] = mm_last(gl, w_out)

        def act(i):
            start = pl.multiple_of(i * 16, 16)
            at, at2 = pl.ds(start, 16), pl.ds(start + segs, 16)
            h, ga = rows_v[at, :], rows_v[at2, :]
            h2 = h * h
            t = jnp.tanh(h * (GELU_A + (GELU_A * GELU_B) * h2))
            half_t = 0.5 + 0.5 * t
            slope = half_t + (0.5 * h) * (1.0 - t * t) * (GELU_A + (3.0 * GELU_A * GELU_B) * h2)
            rows_hi[at, :] = (h * half_t).astype(bf16)
            rows_hi[at2, :] = (ga * slope).astype(bf16)

        each(segs // 16, act)
        active, gh = rows_hi[0:segs, :], rows_hi[segs:2 * segs, :]
        mixed_v[...] += mm(active, w_out)
        gnorm[...] += mm_last(gh, w_in)
        part_in, part_out = mm_first(gh, n2), mm_first(active, gl)
        for c in range(n_cols):
            gw[0, c, at_h, :] = part_in[:, c * 128:(c + 1) * 128]
            gw[1, c, at_h, :] = part_out[:, c * 128:(c + 1) * 128]
        core_copy(j).start()

    each(n_hb, mlp_block)
    store_mixed = pltpu.make_async_copy(mixed_v, mixed_hbm, ld_sem.at[4])
    store_mixed.start()

    small[...] = jnp.zeros(small.shape, f32)

    def norm_back(i):
        at = pl.ds(pl.multiple_of(i * CH, CH), CH)
        g, unit = gnorm[at, :], xhat2[at, :]
        prod = g * unit
        small[...] += fold8(prod)
        dx = g * mgain
        a = jnp.sum(dx, axis=1, keepdims=True) * inv
        b = jnp.sum(prod * mgain, axis=1, keepdims=True) * inv
        gp = gout_v[at, :] + wide(rstd2[at, :]) * (dx - a - unit * b)
        rows_hi[at, :], rows_lo[at, :] = split_hi_lo(gp / wide(plen[at, :]))

    each(segs // CH, norm_back)
    mgain_part = jnp.sum(small[...], axis=0, keepdims=True)
    gc[pl.ds(PAD, count), :] = mm(pool_t[...], rows_hi[0:segs, :]) + mm(pool_t[...], rows_lo[0:segs, :])
    for copy in halo(gc, 2):
        copy.start()

    per = 256
    n_per = hidden // per

    def add_core(i):
        c, k = lax.div(i, n_per), lax.rem(i, n_per)
        at = pl.ds(pl.multiple_of(k * per, per), per)
        gw[core, c, at, :] += rc[c, at, :]

    each(n_hb, lambda j: core_copy(j).wait_recv())
    each(n_cols * n_per, add_core)

    def y_send(o):
        yy = lax.rem(y + o, n_y)
        return remote(gw.at[core, yy], ry.at[o - 1], y_s.at[o - 1], y_r.at[o - 1], yy * 2 + core, me)

    each(n_y, lambda o: y_send(o).start(), 1)

    def back_rows(i):
        base = pl.multiple_of(i * CH, CH)
        own = pl.ds(base + PAD, CH)
        here, unit = sid[own, :], xhat[own, :]
        gl = jnp.zeros((CH, chans), f32)
        around = gc[pl.ds(base, CH + 2 * PAD), :]
        for e in range(-half, half + 1):
            same = wide(ones_where(sid[pl.ds(base + PAD + e, CH), :] == here)) * rows_from(around, PAD + e, CH)
            gl = gl + taps[half - e:half - e + 1, :] * same
            gtap_acc[half - e] += fold8(unit * same)
        dx = gl * cgain
        a = jnp.sum(dx, axis=1, keepdims=True) * inv
        b = jnp.sum(dx * unit, axis=1, keepdims=True) * inv
        gs = gc[own, :] + wide(rstd[own, :]) * (dx - a - unit * b)
        at = pl.ds(base, CH)
        val_hi[at, :], val_lo[at, :] = split_hi_lo(gs)

    each(n_chunks - 1, back_rows, 1)
    for copy in halo(gc, 2):
        copy.wait_recv()
    each(2, lambda i: back_rows(i * (n_chunks - 1)))

    def sent_all(i):
        p = lax.rem(me + i, n_seq)
        row_out(p, outb, inb, row_s, row_r).wait_send()

    each(n_seq, sent_all, 1)
    slot_at = iota_f((slots, count), 0)

    def return_group(g):
        p0 = group_out(g)
        hot = ones_where(slot_at == srow[0:1, :] - (p0 * cap).astype(f32)).astype(bf16)
        made = mm(hot, val_hi[...]) + mm(hot, val_lo[...])
        outb[pl.ds(p0, group)] = made.reshape(group, cap, chans)
        launch(p0, inb2, back_s, back_r)

    each(n_groups, return_group)

    for d in range(2 * half + 1):
        small[d:d + 1, :] = jnp.sum(gtap_acc[d], axis=0, keepdims=True)
    small[7:8, :] = mgain_part
    rs1[dp] = small[...]

    def s1_send(o):
        to = lax.rem(dp + o, n_dp)
        return remote(small, rs1.at[dp], s1_s.at[to], s1_r.at[dp], to, me)

    def s1_recv(o):
        to = lax.rem(dp + o, n_dp)
        return remote(small, rs1.at[to], s1_s.at[to], s1_r.at[to], to, me)

    each(n_dp, lambda o: s1_send(o).start(), 1)

    each(n_y, lambda o: y_send(o).wait_recv(), 1)

    def add_y(i):
        zz = lax.div(i, NX)
        xx = lax.rem(i, NX)
        at = pl.ds(pl.multiple_of(i * 64, 64), 64)
        total = gw[core, y, at, :]
        for o in range(n_y - 1):
            total = total + ry[o, at, :]
        wx[xx, zz] = total

    each(n_z * NX, add_y)
    each(n_dp, lambda o: s1_recv(o).wait_recv(), 1)
    total = rs1[0]
    for i in range(1, n_dp):
        total = total + rs1[i]
    rs2[x] = total

    def x_send(o):
        xx = lax.rem(x + o, NX)
        return remote(wx.at[xx], rx.at[o - 1], x_s.at[o - 1], x_r.at[o - 1], dp, z * NX + xx)

    def s2_send(o):
        xx = lax.rem(x + o, NX)
        return remote(rs2.at[x], rs2.at[x], s2_s.at[xx], s2_r.at[x], dp, z * NX + xx)

    def s2_recv(o):
        xx = lax.rem(x + o, NX)
        return remote(rs2.at[x], rs2.at[xx], s2_s.at[xx], s2_r.at[xx], dp, z * NX + xx)

    each(NX, lambda o: x_send(o).start(), 1)
    each(NX, lambda o: s2_send(o).start(), 1)
    each(NX, lambda o: x_send(o).wait_recv(), 1)

    def add_x(zz):
        total = wx[x, zz]
        for o in range(NX - 1):
            total = total + rx[o, zz]
        wz[zz] = total

    each(n_z, add_x)
    each(NX, lambda o: s2_recv(o).wait_recv(), 1)
    total = rs2[0]
    for i in range(1, NX):
        total = total + rs2[i]
    rs3[z] = total

    def z_send(o):
        zz = lax.rem(z + o, n_z)
        return remote(wz.at[zz], rz.at[o - 1], z_s.at[o - 1], z_r.at[o - 1], dp, zz * NX + x)

    def s3_send(o):
        zz = lax.rem(z + o, n_z)
        return remote(rs3.at[z], rs3.at[z], s3_s.at[zz], s3_r.at[z], dp, zz * NX + x)

    def s3_recv(o):
        zz = lax.rem(z + o, n_z)
        return remote(rs3.at[z], rs3.at[zz], s3_s.at[zz], s3_r.at[zz], dp, zz * NX + x)

    each(n_z, lambda o: z_send(o).start(), 1)
    each(n_z, lambda o: s3_send(o).start(), 1)
    each(n_z, lambda o: z_send(o).wait_recv(), 1)
    total = wz[z]
    for o in range(n_z - 1):
        total = total + rz[o]
    fin[core, y] = total

    def f_send(o):
        to = lax.rem(dp + o, n_dp)
        return remote(fin.at[core, y], fin.at[core, y], f_s.at[to], f_r.at[dp], to, me)

    def f_recv(o):
        to = lax.rem(dp + o, n_dp)
        part = fin.at[lax.rem(to, 2), lax.div(to, 2)]
        return remote(fin.at[core, y], part, f_s.at[to], f_r.at[to], to, me)

    each(n_dp, lambda o: f_send(o).start(), 1)
    each(n_z, lambda o: s3_recv(o).wait_recv(), 1)
    total = rs3[0]
    for i in range(1, n_z):
        total = total + rs3[i]
    gtaps_ref[...] = total[0:2 * half + 1, :] * cgain
    gcg_ref[...] = jnp.sum(total[0:2 * half + 1, :] * taps, axis=0, keepdims=True)
    gmg_ref[...] = total[7:8, :]

    def clear_rows(i):
        rows_v[pl.ds(pl.multiple_of(i * 8, 8), 8), :] = jnp.zeros((8, chans), f32)

    each(count // 8, clear_rows)

    def settle_group(g):
        p0 = group_in(g)
        arrive(p0, inb2, back_s, back_r)
        high, low = split_hi_lo(inb2[pl.ds(p0, group)].reshape(slots, chans))
        hot = pick[pl.ds(pl.multiple_of(p0 * cap, 16), slots), :]
        rows_v[...] += mm_first(hot, high) + mm_first(hot, low)

    each(n_groups, settle_group)
    store_rows = pltpu.make_async_copy(rows_v, grows_hbm, ld_sem.at[5])
    store_rows.start()

    each(n_dp, lambda o: f_recv(o).wait_recv(), 1)
    gwout_ref[...] = jnp.concatenate([fin[1, c] for c in range(n_cols)], axis=1)
    for c in range(n_cols):
        piece = jnp.concatenate([fin[0, c], jnp.zeros((64, 128), f32)], axis=0)
        gwin_ref[c * 128:(c + 1) * 128, :] = jnp.transpose(piece)[:, 0:64]

    each(n_seq, lambda i: send_list(i).wait_send(), 1)

    def back_sent(i):
        p = lax.rem(me + i, n_seq)
        row_out(p, outb, inb2, back_s, back_r).wait_send()

    each(n_seq, back_sent, 1)
    for copy in halo(ser, 0) + halo(gc, 2):
        copy.wait_send()
    each(n_hb, lambda j: core_copy(j).wait_send())
    each(n_y, lambda o: y_send(o).wait_send(), 1)
    each(NX, lambda o: x_send(o).wait_send(), 1)
    each(n_z, lambda o: z_send(o).wait_send(), 1)
    each(n_dp, lambda o: s1_send(o).wait_send(), 1)
    each(NX, lambda o: s2_send(o).wait_send(), 1)
    each(n_z, lambda o: s3_send(o).wait_send(), 1)
    each(n_dp, lambda o: f_send(o).wait_send(), 1)
    store_mixed.wait()
    store_rows.wait()


def make_body(n_dp, n_seq):
    n_y, n_z = n_dp // 2, n_seq // NX

    def body(point_rows, serial_order, scene_counts, pool_counts, conv_gain, conv_kernel, mixer_gain,
             weight_in, weight_out, grad_out):
        count, chans = point_rows.shape
        segs = grad_out.shape[0]
        hidden = weight_out.shape[0]
        cap = 3 * (count // (2 * n_seq))
        share = hidden // n_seq
        pads = count + 2 * PAD
        cols = chans // 128
        V = pltpu.VMEM
        D = lambda n: pltpu.SemaphoreType.DMA((n,))
        any_spec = pl.BlockSpec(memory_space=pl.ANY)
        vmem = pl.BlockSpec(memory_space=pltpu.VMEM)
        shape = jax.ShapeDtypeStruct
        scratch = [
            V((count, chans), f32), V((count, chans), bf16), V((count, chans), bf16),
            V((n_seq, 8, 128), f32), V((n_seq, 8, 128), f32), V((count, 128), bf16),
            V((count, 128), f32), V((8, count), f32), V((128, n_seq * 8), f32), V((n_seq * cap, count), bf16),
            V((n_seq, cap, chans), f32), V((n_seq, cap, chans), f32), V((n_seq, cap, chans), f32),
            V((pads, chans), f32), V((pads, chans), f32), V((pads, 128), f32), V((pads, 128), f32),
            V((count, chans), bf16), V((count, chans), bf16),
            V((segs, count), bf16), V((count, segs), bf16), V((segs, 128), f32),
            V((segs, chans), f32), V((segs, chans), bf16), V((segs, chans), f32), V((segs, chans), f32),
            V((segs, chans), bf16), V((segs, chans), f32), V((segs, 128), f32),
            V((chans, hidden), bf16), V((hidden, chans), bf16),
            V((2, cols, hidden, 128), f32), V((cols, hidden, 128), f32), V((n_y - 1, hidden, 128), f32),
            V((NX, n_z, share, 128), f32), V((NX - 1, n_z, share, 128), f32),
            V((n_z, share, 128), f32), V((n_z - 1, share, 128), f32), V((2, cols, share, 128), f32),
            V((pads, chans), f32), V((8, 8, chans), f32), V((8, chans), f32),
            V((n_dp, 8, chans), f32), V((NX, 8, chans), f32), V((n_z, 8, chans), f32),
            D(6), D(n_seq), D(n_seq), D(n_seq), D(n_seq), D(n_seq), D(n_seq), D(4), D(4),
            D(hidden // 512), D(hidden // 512), D(n_y), D(n_y), D(NX), D(NX), D(n_z), D(n_z),
            D(n_dp), D(n_dp), D(NX), D(NX), D(n_z), D(n_z), D(n_dp), D(n_dp),
        ]
        outs = pl.pallas_call(
            lambda *refs: kernel(n_dp, n_seq, cap, *refs),
            out_shape=(
                shape((segs, chans), f32), shape((count, chans), f32), shape((chans, share), f32),
                shape((share, chans), f32), shape(conv_kernel.shape, f32), shape((1, chans), f32),
                shape((1, chans), f32),
            ),
            in_specs=[any_spec] + [vmem] * 6 + [any_spec] * 3,
            out_specs=(any_spec, any_spec, vmem, vmem, vmem, vmem, vmem),
            scratch_shapes=scratch,
            compiler_params=pltpu.CompilerParams(
                collective_id=0, has_side_effects=True, vmem_limit_bytes=62 * 1024 * 1024),
            name="point_window",
        )(
            point_rows, serial_order, scene_counts, pool_counts.reshape(1, segs), conv_gain[None], conv_kernel,
            mixer_gain[None], weight_in, weight_out, grad_out,
        )
        mixed, grows, gwin, gwout, gtaps, gcg, gmg = outs
        return mixed, grows, gwin, gwout, gtaps, gcg[0], gmg[0]

    return body


def solution(mesh):
    return jax.shard_map(
        make_body(mesh.shape["dp"], mesh.shape["seq"]),
        mesh=mesh,
        in_specs=(
            P(("dp", "seq"), None), P("dp", "seq"), P("dp", None), P("dp", "seq", None), P(), P(), P(), P(), P(),
            P(("dp", "seq"), None),
        ),
        out_specs=(
            P(("dp", "seq"), None), P(("dp", "seq"), None), P(None, "seq"), P("seq", None), P(), P(), P(),
        ),
        check_vma=False,
    )
```

time: 776 us -> 234 us (0.30)
  the two profiles are of different devices: /device:TPU:1 before, /device:TPU:14 now
where the time goes in v1:
time: 234 us
  Pallas kernels  225 us (96%)
  local copies, waits for them, and re-layouts  7.89 us (3%)
    pallas_call x1, Pallas kernels, body(): pl.pallas_call(lambda *refs: kernel(n_dp, n_seq, cap, *refs), out_shape=(...  225 us
    unnamed x17, local copies, waits for them, and re-layouts  7.89 us

profile of v1, /device:TPU:14, one launch (start us, length us, event | category | flops | bytes accessed | tf_op | source)
XLA Modules:
  0.0 233.6 jit_solution(17565941722021653466)
XLA Ops:
  0.6 225.0 %point_window.1 = (f32[512,512]{1,0:T(8,128)}, f32[1024,512]{1,0:T(8,128)}, f32[512,64]{1,0:T(8,128)}, f32[64,512]{1,0:T(8,128)}, f32[7,512]{1,0:T(8,128)}, /*index=5*/f32[1,512]{1,0:T(1,128)}, f32[1,512]{1,0:T(1,128)}) custom-call(f32[1024,512]{1,0:T(8,128)} %refs_0_.1, s32[1,1024]{1,0:T(1,128)} %refs_1_.1, s32[1,64]{1,0:T(1,128)} %refs_2_.1, ...), custom_call_target="tpu_custom_call" | custom-call | tf_op jit(solution)/shard_map/point_window/pallas_call | solution.py:634
  225.7 0.0 copy-start
  225.7 1.9 copy.17
  227.6 2.3 copy.24
  229.8 0.0 copy-done
  229.8 0.0 copy-start.1
  229.8 0.0 copy-start.2
  229.8 0.0 copy-start.4
  229.8 0.0 copy-start.3
  229.8 1.3 copy.25
  231.2 0.0 copy-done.1
  231.2 0.7 copy.26
  231.8 0.0 copy-done.2
  231.8 0.6 copy.27
  232.4 0.0 copy-done.4
  232.4 0.6 copy.28
  233.0 0.0 copy-done.3
  233.0 0.6 copy.29
Async XLA Ops:
  225.7 4.1 %copy-start = (f32[1024,512]{1,0:T(8,128)S(1)}, f32[1024,512]{1,0:T(8,128)}, u32[]{:S(2)}) copy-start(f32[1024,512]{1,0:T(8,128)} %get-tuple-element.36) | copy-start | bytes 6291460
  229.8 1.3 copy-start.1
  229.8 2.0 copy-start.2
  229.8 2.6 %copy-start.4 = (f32[1,512]{1,0:T(1,128)S(1)}, f32[1,512]{1,0:T(1,128)}, u32[]{:S(2)}) copy-start(f32[1,512]{1,0:T(1,128)} %get-tuple-element.19) | copy-start | bytes 6148
  229.8 3.2 %copy-start.3 = (f32[1,512]{1,0:T(1,128)S(1)}, f32[1,512]{1,0:T(1,128)}, u32[]{:S(2)}) copy-start(f32[1,512]{1,0:T(1,128)} %get-tuple-element.20) | copy-start | bytes 6148

commit v2 on v1

--- a/solution.py
+++ b/solution.py
@@ -54,16 +54,19 @@
 
 
 def kernel(
-    n_dp, n_seq, cap,
+    n_dp, n_seq, cap, spare,
     rows_hbm, order_ref, scene_ref, pool_ref, cgain_ref, taps_ref, mgain_ref, win_hbm, wout_hbm, gout_hbm,
-    mixed_hbm, grows_hbm, gwin_ref, gwout_ref, gtaps_ref, gcg_ref, gmg_ref,
+    mixed_hbm, grows_hbm, gwin_ref, gwout_ref, gtaps_ref, gcg_ref, gmg_ref, misfit_ref,
     rows_v, rows_hi, rows_lo, list_s, list_r, kmat, scol, srow, tcol, pick,
     outb, inb, inb2, ser, xhat, rstd, sid, val_hi, val_lo,
     pool_m, pool_t, plen, gout_v, glow, mixed_v, xhat2, norm2, gnorm, rstd2,
     win_v, wout_v, gw, rc, ry, wx, rx, wz, rz, fin, gc, gtap_acc, small, rs1, rs2, rs3,
     ld_sem, idx_s, idx_r, row_s, row_r, back_s, back_r, halo_s, halo_r,
-    core_s, core_r, y_s, y_r, x_s, x_r, z_s, z_r, s1_s, s1_r, s2_s, s2_r, s3_s, s3_r, f_s, f_r,
+    core_s, core_r, y_s, y_r, x_s, x_r, z_s, z_r, s1_s, s1_r, s2_s, s2_r, s3_s, s3_r, f_s, f_r, *extra,
 ):
+    if spare:
+        ocol, orow, pick2, hop_a, hop_b, hop_c, hop_d, ret_a, ret_b, ret_c, ret_d = extra[:11]
+        hop1_s, hop1_r, hop2_s, hop2_r, ret1_s, ret1_r, ret2_s, ret2_r = extra[11:]
     count, chans = rows_v.shape
     segs = mixed_v.shape[0]
     hidden = wout_v.shape[0]
@@ -119,9 +122,17 @@
         ranks = mm(below, hot.astype(bf16)) + before
         before = before + jnp.sum(hot, axis=0, keepdims=True)
         rank = jnp.broadcast_to(jnp.sum(hot * ranks, axis=1, keepdims=True), (128, 128))
-        scol[b * 128:(b + 1) * 128, :] = own_b * cap + rank
+        slot = own_b * cap + rank
+        if spare:
+            via = rank + (me + 1 - cap).astype(f32)
+            via = jnp.where(via >= n_seq, via - n_seq, via)
+            ocol[b * 128:(b + 1) * 128, :] = jnp.where(rank >= cap, via, -1.0)
+            slot = jnp.where(rank >= cap, -1.0, slot)
+        scol[b * 128:(b + 1) * 128, :] = slot
         kmat[b * 128:(b + 1) * 128, :] = ones_where(rank == lane).astype(bf16)
     srow[...] = jnp.transpose(scol[...])[0:8, :]
+    if spare:
+        orow[...] = jnp.transpose(ocol[...])[0:8, :]
     owner_hot = ones_where(jnp.broadcast_to(owner, (n_seq, count)) == iota_f((n_seq, count), 0))
     kval = kmat[...]
     lists = (
@@ -130,6 +141,16 @@
         + mm(owner_hot.astype(bf16), kval)
         - 1.0
     )
+    misfit = jnp.zeros((1, 1), f32)
+    if spare:
+        over = ones_where(before > cap)
+        over_n = jnp.sum(jnp.maximum(before - cap, 0.0), axis=1, keepdims=True)
+        over_from = jnp.sum(over * lane[0:1], axis=1, keepdims=True)
+        misfit = misfit + ones_where(jnp.sum(over, axis=1, keepdims=True) > 1.0)
+        place = iota_f((n_seq, 128), 0) - (me + 1).astype(f32)
+        place = jnp.where(place < 0.0, place + n_seq, place)
+        passed = jnp.where(place < over_n, over_from, -1.0)
+        lists = jnp.where(iota_f((n_seq, 128), 1) == 64.0, passed, lists)
     for p in range(n_seq):
         list_s[p] = jnp.broadcast_to(lists[p:p + 1, :], (8, 128))
     list_r[me] = list_s[me]
@@ -156,6 +177,46 @@
     each(n_seq, lambda i: recv_list(i).wait_recv(), 1)
 
     tcol[...] = jnp.transpose(list_r[...].reshape(n_seq * 8, 128))
+
+    def hop_out(i, src, dst, send, recv):
+        p = lax.rem(me + i, n_seq)
+        return remote(src.at[p], dst.at[me], send.at[p], recv.at[me], dp, p)
+
+    def hop_in(i, src, dst, send, recv):
+        p = lax.rem(me + i, n_seq)
+        return remote(src.at[p], dst.at[p], send.at[p], recv.at[p], dp, p)
+
+    def hop_send(value, src, dst, send, recv):
+        for p in range(n_seq):
+            src[p] = value[p:p + 1, :]
+        dst[me] = src[me]
+        each(n_seq, lambda i: hop_out(i, src, dst, send, recv).start(), 1)
+
+    def hop_read(src, dst, send, recv):
+        each(n_seq, lambda i: hop_in(i, src, dst, send, recv).wait_recv(), 1)
+        return split_hi_lo(jnp.concatenate([dst[p] for p in range(n_seq)], axis=0))
+
+    if spare:
+        flat = list_r[...].reshape(n_seq * 8, 128)
+        wanted = jnp.max(flat, axis=0, keepdims=True)
+        blocks = lax.broadcasted_iota(jnp.int32, (1, n_seq * 8), 1)
+        busy = tcol[cap:cap + 1, :] >= 0.0
+        over_to = jnp.max(jnp.where(busy, (blocks >> 3).astype(f32), -1.0), axis=1, keepdims=True)
+        misfit = misfit + ones_where(jnp.sum(ones_where(busy), axis=1, keepdims=True) > 8.0)
+        place = iota_f((n_seq, 128), 0) - 1.0 - over_to
+        place = jnp.where(place < 0.0, place + n_seq, place)
+        col = jnp.sum(jnp.where(iota_f((n_seq, 128), 1) == place + cap, wanted + 1.0, 0.0), axis=1, keepdims=True) - 1.0
+        pick2[...] = ones_where(jnp.broadcast_to(col, (n_seq, count)) == iota_f((n_seq, count), 1)).astype(bf16)
+        hop1 = (hop_a, hop_b, hop1_s, hop1_r)
+        hop2 = (hop_c, hop_d, hop2_s, hop2_r)
+        ret1 = (ret_a, ret_b, ret1_s, ret1_r)
+        ret2 = (ret_c, ret_d, ret2_s, ret2_r)
+        hop_send(mm(pick2[...], rows_hi[...]) + mm(pick2[...], rows_lo[...]), *hop1)
+        rows_of = jnp.max(list_r[...], axis=1)
+        passed_from = jnp.sum(
+            jnp.where(iota_f((n_seq, 128), 1) == 64.0, rows_of, 0.0), axis=1, keepdims=True)
+        pass_on = ones_where(
+            jnp.broadcast_to(passed_from, (n_seq, n_seq)) == iota_f((n_seq, n_seq), 1)).astype(bf16)
 
     def row_out(p, src, dst, send, recv):
         return remote(src.at[p], dst.at[me], send.at[p], recv.at[me], dp, p)
@@ -212,7 +273,13 @@
         outb[pl.ds(p0, group)] = made.reshape(group, cap, chans)
         launch(p0, inb, row_s, row_r)
 
-    each(n_groups, gather_group)
+    if spare:
+        each(n_groups // 2, gather_group)
+        high, low = hop_read(*hop1)
+        hop_send(mm(pass_on, high) + mm(pass_on, low), *hop2)
+        each(n_groups, gather_group, n_groups // 2)
+    else:
+        each(n_groups, gather_group)
 
     scene_n = scene_ref.shape[1]
     upto = ones_where(iota_f((scene_n, scene_n), 0) <= iota_f((scene_n, scene_n), 1))
@@ -267,6 +334,10 @@
         ser[pl.ds(PAD, count), :] += mm(hot, high) + mm(hot, low)
 
     each(n_groups, place_group)
+    if spare:
+        high, low = hop_read(*hop2)
+        hot = ones_where(ocol[:, 0:n_seq] == iota_f((count, n_seq), 1)).astype(bf16)
+        ser[pl.ds(PAD, count), :] += mm(hot, high) + mm(hot, low)
 
     right, left = lax.rem(me + 1, n_seq), lax.rem(me + n_seq - 1, n_seq)
 
@@ -383,7 +454,7 @@
         at = pl.ds(pl.multiple_of(i * CH, CH), CH)
         g, unit = gnorm[at, :], xhat2[at, :]
         prod = g * unit
-        small[...] += fold8(prod)
+        small[0:8, :] += fold8(prod)
         dx = g * mgain
         a = jnp.sum(dx, axis=1, keepdims=True) * inv
         b = jnp.sum(prod * mgain, axis=1, keepdims=True) * inv
@@ -391,7 +462,7 @@
         rows_hi[at, :], rows_lo[at, :] = split_hi_lo(gp / wide(plen[at, :]))
 
     each(segs // CH, norm_back)
-    mgain_part = jnp.sum(small[...], axis=0, keepdims=True)
+    mgain_part = jnp.sum(small[0:8, :], axis=0, keepdims=True)
     gc[pl.ds(PAD, count), :] = mm(pool_t[...], rows_hi[0:segs, :]) + mm(pool_t[...], rows_lo[0:segs, :])
     for copy in halo(gc, 2):
         copy.start()
@@ -449,11 +520,21 @@
         outb[pl.ds(p0, group)] = made.reshape(group, cap, chans)
         launch(p0, inb2, back_s, back_r)
 
-    each(n_groups, return_group)
+    if spare:
+        hot = ones_where(
+            jnp.broadcast_to(orow[0:1, :], (n_seq, count)) == iota_f((n_seq, count), 0)).astype(bf16)
+        hop_send(mm(hot, val_hi[...]) + mm(hot, val_lo[...]), *ret1)
+        each(n_groups // 2, return_group)
+        high, low = hop_read(*ret1)
+        hop_send(mm_first(pass_on, high) + mm_first(pass_on, low), *ret2)
+        each(n_groups, return_group, n_groups // 2)
+    else:
+        each(n_groups, return_group)
 
     for d in range(2 * half + 1):
         small[d:d + 1, :] = jnp.sum(gtap_acc[d], axis=0, keepdims=True)
     small[7:8, :] = mgain_part
+    small[8:16, :] = jnp.broadcast_to(misfit, (8, chans))
     rs1[dp] = small[...]
 
     def s1_send(o):
@@ -550,6 +631,7 @@
     gtaps_ref[...] = total[0:2 * half + 1, :] * cgain
     gcg_ref[...] = jnp.sum(total[0:2 * half + 1, :] * taps, axis=0, keepdims=True)
     gmg_ref[...] = total[7:8, :]
+    misfit_ref[...] = total[8:16, 0:128]
 
     def clear_rows(i):
         rows_v[pl.ds(pl.multiple_of(i * 8, 8), 8), :] = jnp.zeros((8, chans), f32)
@@ -564,6 +646,9 @@
         rows_v[...] += mm_first(hot, high) + mm_first(hot, low)
 
     each(n_groups, settle_group)
+    if spare:
+        high, low = hop_read(*ret2)
+        rows_v[...] += mm_first(pick2[...], high) + mm_first(pick2[...], low)
     store_rows = pltpu.make_async_copy(rows_v, grows_hbm, ld_sem.at[5])
     store_rows.start()
 
@@ -590,6 +675,9 @@
     each(NX, lambda o: s2_send(o).wait_send(), 1)
     each(n_z, lambda o: s3_send(o).wait_send(), 1)
     each(n_dp, lambda o: f_send(o).wait_send(), 1)
+    if spare:
+        for hop in (hop1, hop2, ret1, ret2):
+            each(n_seq, lambda i: hop_out(i, *hop).wait_send(), 1)
     store_mixed.wait()
     store_rows.wait()
 
@@ -602,7 +690,7 @@
         count, chans = point_rows.shape
         segs = grad_out.shape[0]
         hidden = weight_out.shape[0]
-        cap = 3 * (count // (2 * n_seq))
+        even = count // n_seq
         share = hidden // n_seq
         pads = count + 2 * PAD
         cols = chans // 128
@@ -611,7 +699,7 @@
         any_spec = pl.BlockSpec(memory_space=pl.ANY)
         vmem = pl.BlockSpec(memory_space=pltpu.VMEM)
         shape = jax.ShapeDtypeStruct
-        scratch = [
+        scratch = lambda cap: [
             V((count, chans), f32), V((count, chans), bf16), V((count, chans), bf16),
             V((n_seq, 8, 128), f32), V((n_seq, 8, 128), f32), V((count, 128), bf16),
             V((count, 128), f32), V((8, count), f32), V((128, n_seq * 8), f32), V((n_seq * cap, count), bf16),
@@ -625,29 +713,37 @@
             V((2, cols, hidden, 128), f32), V((cols, hidden, 128), f32), V((n_y - 1, hidden, 128), f32),
             V((NX, n_z, share, 128), f32), V((NX - 1, n_z, share, 128), f32),
             V((n_z, share, 128), f32), V((n_z - 1, share, 128), f32), V((2, cols, share, 128), f32),
-            V((pads, chans), f32), V((8, 8, chans), f32), V((8, chans), f32),
-            V((n_dp, 8, chans), f32), V((NX, 8, chans), f32), V((n_z, 8, chans), f32),
+            V((pads, chans), f32), V((8, 8, chans), f32), V((16, chans), f32),
+            V((n_dp, 16, chans), f32), V((NX, 16, chans), f32), V((n_z, 16, chans), f32),
             D(6), D(n_seq), D(n_seq), D(n_seq), D(n_seq), D(n_seq), D(n_seq), D(4), D(4),
             D(hidden // 512), D(hidden // 512), D(n_y), D(n_y), D(NX), D(NX), D(n_z), D(n_z),
             D(n_dp), D(n_dp), D(NX), D(NX), D(n_z), D(n_z), D(n_dp), D(n_dp),
         ]
-        outs = pl.pallas_call(
-            lambda *refs: kernel(n_dp, n_seq, cap, *refs),
-            out_shape=(
-                shape((segs, chans), f32), shape((count, chans), f32), shape((chans, share), f32),
-                shape((share, chans), f32), shape(conv_kernel.shape, f32), shape((1, chans), f32),
-                shape((1, chans), f32),
-            ),
-            in_specs=[any_spec] + [vmem] * 6 + [any_spec] * 3,
-            out_specs=(any_spec, any_spec, vmem, vmem, vmem, vmem, vmem),
-            scratch_shapes=scratch,
-            compiler_params=pltpu.CompilerParams(
-                collective_id=0, has_side_effects=True, vmem_limit_bytes=62 * 1024 * 1024),
-            name="point_window",
-        )(
-            point_rows, serial_order, scene_counts, pool_counts.reshape(1, segs), conv_gain[None], conv_kernel,
-            mixer_gain[None], weight_in, weight_out, grad_out,
-        )
+        hop = [V((n_seq, 1, chans), f32)] * 8
+        extra = [V((count, 128), f32), V((8, count), f32), V((n_seq, count), bf16)] + hop + [D(n_seq)] * 8
+
+        def call(cap, spare, ident, name):
+            return pl.pallas_call(
+                lambda *refs: kernel(n_dp, n_seq, cap, spare, *refs),
+                out_shape=(
+                    shape((segs, chans), f32), shape((count, chans), f32), shape((chans, share), f32),
+                    shape((share, chans), f32), shape(conv_kernel.shape, f32), shape((1, chans), f32),
+                    shape((1, chans), f32), shape((8, 128), f32),
+                ),
+                in_specs=[any_spec] + [vmem] * 6 + [any_spec] * 3,
+                out_specs=(any_spec, any_spec, vmem, vmem, vmem, vmem, vmem, vmem),
+                scratch_shapes=scratch(cap) + (extra if spare else []),
+                compiler_params=pltpu.CompilerParams(
+                    collective_id=ident, has_side_effects=True, vmem_limit_bytes=62 * 1024 * 1024),
+                name=name,
+            )(
+                point_rows, serial_order, scene_counts, pool_counts.reshape(1, segs), conv_gain[None], conv_kernel,
+                mixer_gain[None], weight_in, weight_out, grad_out,
+            )
+
+        outs = call(even, even // 2, 0, "window_even")
+        outs = lax.cond(
+            outs[7][0, 0] > 0.0, lambda: call(even + even // 2, 0, 1, "window_full")[:7], lambda: outs[:7])
         mixed, grows, gwin, gwout, gtaps, gcg, gmg = outs
         return mixed, grows, gwin, gwout, gtaps, gcg[0], gmg[0]
 

time: 234 us -> 211 us (0.902)
  the two profiles are of different devices: /device:TPU:14 before, /device:TPU:1 now
where the time goes in v2:
time: 211 us
  Pallas kernels  202 us (96%)
  local copies, waits for them, and re-layouts  7.99 us (4%)
    pallas_call x1, Pallas kernels, call(): pl.pallas_call(lambda *refs: kernel(n_dp, n_seq, cap, spare, *refs), out_...  202 us
    unnamed x23, local copies, waits for them, and re-layouts  6.8 us

profile of v2, /device:TPU:1, one launch (start us, length us, event | category | flops | bytes accessed | tf_op | source)
XLA Modules:
  0.0 211.1 jit_solution(309164389527601910)
XLA Ops:
  0.6 0.0 copy-start
  0.6 0.0 copy-start.2
  0.7 0.0 copy-start.3
  0.7 0.0 copy-start.4
  0.7 0.0 copy-start.5
  0.7 0.0 copy-start.6
  0.7 0.0 copy-start.7
  0.7 201.5 %window_even.1 = (f32[512,512]{1,0:T(8,128)}, f32[1024,512]{1,0:T(8,128)}, f32[512,64]{1,0:T(8,128)S(1)}, f32[64,512]{1,0:T(8,128)S(1)}, f32[7,512]{1,0:T(8,128)...) custom-call(f32[1024,512]{1,0:T(8,128)} %refs_0_.1, s32[1,1024]{1,0:T(1,128)} %refs_1_.1, ...), custom_call_target="tpu_custom_call" | custom-call | tf_op jit(solution)/shard_map/window_even/pallas_call | solution.py:726
  202.2 1.2 slice.3
  204.1 0.0 copy-done
  204.1 0.0 copy-done.2
  204.1 0.0 copy-done.3
  204.1 0.0 copy-done.4
  204.1 0.0 copy-done.5
  204.1 0.0 copy-done.6
  204.1 0.0 copy-done.7
  204.2 0.2 conditional.1
  204.4 0.0 copy-start.1
  204.4 0.8 copy.17
  205.1 2.3 %copy.38 = f32[512,512]{1,0:T(8,128)} copy(f32[512,512]{1,0:T(8,128)} %get-tuple-element.125) | data formatting | bytes 2097152
  207.4 0.0 copy-done.1
  207.4 1.3 copy.39
  208.7 0.7 copy.40
  209.4 0.6 copy.41
  210.0 0.6 copy.42
  210.6 0.6 copy.43
Async XLA Ops:
  0.6 203.5 %copy-start = (f32[512,512]{1,0:T(8,128)S(1)}, f32[512,512]{1,0:T(8,128)}, u32[]{:S(2)}) copy-start(f32[512,512]{1,0:T(8,128)} %refs_9_.1) | copy-start | bytes 3145732
  0.6 203.5 %copy-start.2 = (f32[7,512]{1,0:T(8,128)S(1)}, f32[7,512]{1,0:T(8,128)}, u32[]{:S(2)}) copy-start(f32[7,512]{1,0:T(8,128)} %refs_5_.1) | copy-start | bytes 43012
  0.7 203.5 %copy-start.3 = (s32[1,1024]{1,0:T(1,128)S(1)}, s32[1,1024]{1,0:T(1,128)}, u32[]{:S(2)}) copy-start(s32[1,1024]{1,0:T(1,128)} %refs_1_.1) | copy-start | bytes 12292
  0.7 203.5 %copy-start.4 = (s32[1,1,512]{2,1,0:T(1,128)S(1)}, s32[1,1,512]{2,1,0:T(1,128)}, u32[]{:S(2)}) copy-start(s32[1,1,512]{2,1,0:T(1,128)} %param.15) | copy-start | bytes 6148
  0.7 203.5 %copy-start.5 = (f32[512]{0:T(512)S(1)}, f32[512]{0:T(512)}, u32[]{:S(2)}) copy-start(f32[512]{0:T(512)} %param.16) | copy-start | bytes 6148
  0.7 203.5 %copy-start.6 = (f32[512]{0:T(512)S(1)}, f32[512]{0:T(512)}, u32[]{:S(2)}) copy-start(f32[512]{0:T(512)} %param.18) | copy-start | bytes 6148
  0.7 203.5 %copy-start.7 = (s32[1,64]{1,0:T(1,128)S(1)}, s32[1,64]{1,0:T(1,128)}, u32[]{:S(2)}) copy-start(s32[1,64]{1,0:T(1,128)} %refs_2_.1) | copy-start | bytes 772
  204.4 3.0 %copy-start.1 = (f32[1024,512]{1,0:T(8,128)S(1)}, f32[1024,512]{1,0:T(8,128)}, u32[]{:S(2)}) copy-start(f32[1024,512]{1,0:T(8,128)} %get-tuple-element.126) | copy-start | bytes 6291460

commit v3 on v2

--- a/solution.py
+++ b/solution.py
@@ -57,8 +57,8 @@
     n_dp, n_seq, cap, spare,
     rows_hbm, order_ref, scene_ref, pool_ref, cgain_ref, taps_ref, mgain_ref, win_hbm, wout_hbm, gout_hbm,
     mixed_hbm, grows_hbm, gwin_ref, gwout_ref, gtaps_ref, gcg_ref, gmg_ref, misfit_ref,
-    rows_v, rows_hi, rows_lo, list_s, list_r, kmat, scol, srow, tcol, pick,
-    outb, inb, inb2, ser, xhat, rstd, sid, val_hi, val_lo,
+    rows_v, rows_hl, list_s, list_r, kmat, scol, srow, tcol, pick,
+    outb, inb, inb2, ser, xhat, rstd, sid, val_hl,
     pool_m, pool_t, plen, gout_v, glow, mixed_v, xhat2, norm2, gnorm, rstd2,
     win_v, wout_v, gw, rc, ry, wx, rx, wz, rz, fin, gc, gtap_acc, small, rs1, rs2, rs3,
     ld_sem, idx_s, idx_r, row_s, row_r, back_s, back_r, halo_s, halo_r,
@@ -69,6 +69,8 @@
         hop1_s, hop1_r, hop2_s, hop2_r, ret1_s, ret1_r, ret2_s, ret2_r = extra[11:]
     count, chans = rows_v.shape
     segs = mixed_v.shape[0]
+    rows_hi, rows_lo = rows_hl.at[pl.ds(0, count)], rows_hl.at[pl.ds(count, count)]
+    val_hi, val_lo = val_hl.at[pl.ds(0, count)], val_hl.at[pl.ds(count, count)]
     hidden = wout_v.shape[0]
     n_y, n_z = n_dp // 2, n_seq // NX
     group = 8
@@ -401,7 +403,6 @@
         norm2[at, :] = (unit * mgain).astype(bf16)
         rstd2[at, :] = jnp.broadcast_to(r, (CH, 128))
         glow[at, :] = gout_v[at, :].astype(bf16)
-        gnorm[at, :] = jnp.zeros((CH, chans), f32)
 
     each(segs // CH, norm_pooled)
     loads[1].wait()
@@ -431,22 +432,48 @@
             t = jnp.tanh(h * (GELU_A + (GELU_A * GELU_B) * h2))
             half_t = 0.5 + 0.5 * t
             slope = half_t + (0.5 * h) * (1.0 - t * t) * (GELU_A + (3.0 * GELU_A * GELU_B) * h2)
-            rows_hi[at, :] = (h * half_t).astype(bf16)
-            rows_hi[at2, :] = (ga * slope).astype(bf16)
+            at_b = pl.ds(pl.multiple_of(start + j * segs, 16), 16)
+            rows_hl[at_b, :] = (h * half_t).astype(bf16)
+            val_hl[at_b, :] = (ga * slope).astype(bf16)
 
         each(segs // 16, act)
-        active, gh = rows_hi[0:segs, :], rows_hi[segs:2 * segs, :]
-        mixed_v[...] += mm(active, w_out)
-        gnorm[...] += mm_last(gh, w_in)
-        part_in, part_out = mm_first(gh, n2), mm_first(active, gl)
+        at_j = pl.ds(pl.multiple_of(j * segs, segs), segs)
+        part_in, part_out = mm_first(val_hl[at_j, :], n2), mm_first(rows_hl[at_j, :], gl)
         for c in range(n_cols):
             gw[0, c, at_h, :] = part_in[:, c * 128:(c + 1) * 128]
             gw[1, c, at_h, :] = part_out[:, c * 128:(c + 1) * 128]
         core_copy(j).start()
 
-    each(n_hb, mlp_block)
-    store_mixed = pltpu.make_async_copy(mixed_v, mixed_hbm, ld_sem.at[4])
-    store_mixed.start()
+    per = 256
+    n_per = hb // per
+
+    def y_send(j, o):
+        yy = lax.rem(y + o, n_y)
+        at = pl.ds(pl.multiple_of(j * hb, hb), hb)
+        k = j * n_y + o - 1
+        return remote(gw.at[core, yy, at, :], ry.at[o - 1, at, :], y_s.at[k], y_r.at[k], yy * 2 + core, me)
+
+    def core_done(j):
+        core_copy(j).wait_recv()
+
+        def add_core(i):
+            c, k = lax.div(i, n_per), lax.rem(i, n_per)
+            at = pl.ds(pl.multiple_of(j * hb + k * per, per), per)
+            gw[core, c, at, :] += rc[c, at, :]
+
+        each(n_cols * n_per, add_core)
+        each(n_y, lambda o: y_send(j, o).start(), 1)
+
+    def mlp_step(j):
+        mlp_block(j)
+
+        @pl.when(j > 0)
+        def _():
+            core_done(j - 1)
+
+    each(n_hb, mlp_step)
+    gnorm[...] = sum(
+        mm_last(val_hl[j * segs:(j + 1) * segs, :], win_v[:, j * hb:(j + 1) * hb]) for j in range(n_hb))
 
     small[...] = jnp.zeros(small.shape, f32)
 
@@ -459,30 +486,15 @@
         a = jnp.sum(dx, axis=1, keepdims=True) * inv
         b = jnp.sum(prod * mgain, axis=1, keepdims=True) * inv
         gp = gout_v[at, :] + wide(rstd2[at, :]) * (dx - a - unit * b)
-        rows_hi[at, :], rows_lo[at, :] = split_hi_lo(gp / wide(plen[at, :]))
+        val_hi[at, :], val_lo[at, :] = split_hi_lo(gp / wide(plen[at, :]))
 
     each(segs // CH, norm_back)
     mgain_part = jnp.sum(small[0:8, :], axis=0, keepdims=True)
-    gc[pl.ds(PAD, count), :] = mm(pool_t[...], rows_hi[0:segs, :]) + mm(pool_t[...], rows_lo[0:segs, :])
+    gc[pl.ds(PAD, count), :] = mm(pool_t[...], val_hi[0:segs, :]) + mm(pool_t[...], val_lo[0:segs, :])
     for copy in halo(gc, 2):
         copy.start()
 
-    per = 256
-    n_per = hidden // per
-
-    def add_core(i):
-        c, k = lax.div(i, n_per), lax.rem(i, n_per)
-        at = pl.ds(pl.multiple_of(k * per, per), per)
-        gw[core, c, at, :] += rc[c, at, :]
-
-    each(n_hb, lambda j: core_copy(j).wait_recv())
-    each(n_cols * n_per, add_core)
-
-    def y_send(o):
-        yy = lax.rem(y + o, n_y)
-        return remote(gw.at[core, yy], ry.at[o - 1], y_s.at[o - 1], y_r.at[o - 1], yy * 2 + core, me)
-
-    each(n_y, lambda o: y_send(o).start(), 1)
+    core_done(n_hb - 1)
 
     def back_rows(i):
         base = pl.multiple_of(i * CH, CH)
@@ -547,28 +559,40 @@
 
     each(n_dp, lambda o: s1_send(o).start(), 1)
 
-    each(n_y, lambda o: y_send(o).wait_recv(), 1)
-
-    def add_y(i):
-        zz = lax.div(i, NX)
-        xx = lax.rem(i, NX)
-        at = pl.ds(pl.multiple_of(i * 64, 64), 64)
-        total = gw[core, y, at, :]
-        for o in range(n_y - 1):
-            total = total + ry[o, at, :]
-        wx[xx, zz] = total
-
-    each(n_z * NX, add_y)
+    mixed_v[...] += sum(
+        mm(rows_hl[j * segs:(j + 1) * segs, :], wout_v[j * hb:(j + 1) * hb, :]) for j in range(n_hb))
+    store_mixed = pltpu.make_async_copy(mixed_v, mixed_hbm, ld_sem.at[4])
+    store_mixed.start()
+
+    share = hidden // n_seq
+    z_per = n_z // n_hb
+
+    def x_send(j, o):
+        xx = lax.rem(x + o, NX)
+        at, k = pl.ds(j * z_per, z_per), j * NX + o - 1
+        return remote(wx.at[xx, at], rx.at[o - 1, at], x_s.at[k], x_r.at[k], dp, z * NX + xx)
+
+    def y_done(j):
+        each(n_y, lambda o: y_send(j, o).wait_recv(), 1)
+
+        def add_y(i):
+            zz, xx = j * z_per + lax.div(i, NX), lax.rem(i, NX)
+            at = pl.ds(pl.multiple_of((zz * NX + xx) * share, share), share)
+            total = gw[core, y, at, :]
+            for o in range(n_y - 1):
+                total = total + ry[o, at, :]
+            wx[xx, zz] = total
+
+        each(z_per * NX, add_y)
+        each(NX, lambda o: x_send(j, o).start(), 1)
+
+    each(n_hb, y_done)
     each(n_dp, lambda o: s1_recv(o).wait_recv(), 1)
     total = rs1[0]
     for i in range(1, n_dp):
         total = total + rs1[i]
     rs2[x] = total
 
-    def x_send(o):
-        xx = lax.rem(x + o, NX)
-        return remote(wx.at[xx], rx.at[o - 1], x_s.at[o - 1], x_r.at[o - 1], dp, z * NX + xx)
-
     def s2_send(o):
         xx = lax.rem(x + o, NX)
         return remote(rs2.at[x], rs2.at[x], s2_s.at[xx], s2_r.at[x], dp, z * NX + xx)
@@ -577,9 +601,8 @@
         xx = lax.rem(x + o, NX)
         return remote(rs2.at[x], rs2.at[xx], s2_s.at[xx], s2_r.at[xx], dp, z * NX + xx)
 
-    each(NX, lambda o: x_send(o).start(), 1)
     each(NX, lambda o: s2_send(o).start(), 1)
-    each(NX, lambda o: x_send(o).wait_recv(), 1)
+    each(n_hb, lambda j: each(NX, lambda o: x_send(j, o).wait_recv(), 1))
 
     def add_x(zz):
         total = wx[x, zz]
@@ -668,8 +691,8 @@
     for copy in halo(ser, 0) + halo(gc, 2):
         copy.wait_send()
     each(n_hb, lambda j: core_copy(j).wait_send())
-    each(n_y, lambda o: y_send(o).wait_send(), 1)
-    each(NX, lambda o: x_send(o).wait_send(), 1)
+    each(n_hb, lambda j: each(n_y, lambda o: y_send(j, o).wait_send(), 1))
+    each(n_hb, lambda j: each(NX, lambda o: x_send(j, o).wait_send(), 1))
     each(n_z, lambda o: z_send(o).wait_send(), 1)
     each(n_dp, lambda o: s1_send(o).wait_send(), 1)
     each(NX, lambda o: s2_send(o).wait_send(), 1)
@@ -700,12 +723,12 @@
         vmem = pl.BlockSpec(memory_space=pltpu.VMEM)
         shape = jax.ShapeDtypeStruct
         scratch = lambda cap: [
-            V((count, chans), f32), V((count, chans), bf16), V((count, chans), bf16),
+            V((count, chans), f32), V((2 * count, chans), bf16),
             V((n_seq, 8, 128), f32), V((n_seq, 8, 128), f32), V((count, 128), bf16),
             V((count, 128), f32), V((8, count), f32), V((128, n_seq * 8), f32), V((n_seq * cap, count), bf16),
             V((n_seq, cap, chans), f32), V((n_seq, cap, chans), f32), V((n_seq, cap, chans), f32),
             V((pads, chans), f32), V((pads, chans), f32), V((pads, 128), f32), V((pads, 128), f32),
-            V((count, chans), bf16), V((count, chans), bf16),
+            V((2 * count, chans), bf16),
             V((segs, count), bf16), V((count, segs), bf16), V((segs, 128), f32),
             V((segs, chans), f32), V((segs, chans), bf16), V((segs, chans), f32), V((segs, chans), f32),
             V((segs, chans), bf16), V((segs, chans), f32), V((segs, 128), f32),
@@ -716,7 +739,7 @@
             V((pads, chans), f32), V((8, 8, chans), f32), V((16, chans), f32),
             V((n_dp, 16, chans), f32), V((NX, 16, chans), f32), V((n_z, 16, chans), f32),
             D(6), D(n_seq), D(n_seq), D(n_seq), D(n_seq), D(n_seq), D(n_seq), D(4), D(4),
-            D(hidden // 512), D(hidden // 512), D(n_y), D(n_y), D(NX), D(NX), D(n_z), D(n_z),
+            D(hidden // 512), D(hidden // 512), D(4 * n_y), D(4 * n_y), D(4 * NX), D(4 * NX), D(n_z), D(n_z),
             D(n_dp), D(n_dp), D(NX), D(NX), D(n_z), D(n_z), D(n_dp), D(n_dp),
         ]
         hop = [V((n_seq, 1, chans), f32)] * 8

time: 211 us -> 204 us (0.967)
  Pallas kernels: 202 us -> 194 us
    pallas_call x1, Pallas kernels: 202 us -> 194 us  [call(): pl.pallas_call(lambda *refs: kernel(n_dp, n_seq, cap, spare, *refs), out_...]
where the time goes in v3:
time: 204 us; the launch traced here: 203 us
  Pallas kernels  194 us (95%)
  local copies, waits for them, and re-layouts  7.99 us (4%)
    pallas_call x1, Pallas kernels, call(): pl.pallas_call(lambda *refs: kernel(n_dp, n_seq, cap, spare, *refs), out_...  194 us
    unnamed x23, local copies, waits for them, and re-layouts  6.8 us

profile of v3, /device:TPU:1, one launch (start us, length us, event | category | flops | bytes accessed | tf_op | source)
XLA Modules:
  0.0 203.5 jit_solution(11084496369725661899)
XLA Ops:
  0.6 0.0 copy-start
  0.6 0.0 copy-start.2
  0.7 0.0 copy-start.3
  0.7 0.0 copy-start.4
  0.7 0.0 copy-start.5
  0.7 0.0 copy-start.6
  0.7 0.0 copy-start.7
  0.7 194.0 %window_even.1 = (f32[512,512]{1,0:T(8,128)}, f32[1024,512]{1,0:T(8,128)}, f32[512,64]{1,0:T(8,128)S(1)}, f32[64,512]{1,0:T(8,128)S(1)}, f32[7,512]{1,0:T(8,128)...) custom-call(f32[1024,512]{1,0:T(8,128)} %refs_0_.1, s32[1,1024]{1,0:T(1,128)} %refs_1_.1, ...), custom_call_target="tpu_custom_call" | custom-call | tf_op jit(solution)/shard_map/window_even/pallas_call | solution.py:749
  194.8 1.2 slice.3
  196.6 0.0 copy-done
  196.6 0.0 copy-done.2
  196.6 0.0 copy-done.3
  196.6 0.0 copy-done.4
  196.6 0.0 copy-done.5
  196.6 0.0 copy-done.6
  196.7 0.0 copy-done.7
  196.7 0.0 copy-start.1
  196.7 0.8 copy.17
  197.5 2.3 %copy.38 = f32[512,512]{1,0:T(8,128)} copy(f32[512,512]{1,0:T(8,128)} %get-tuple-element.125) | data formatting | bytes 2097152
  199.7 0.0 copy-done.1
  199.7 1.3 copy.39
  201.1 0.7 copy.40
  201.7 0.6 copy.41
  202.3 0.6 copy.42
  202.9 0.6 copy.43
  (1 shorter events, 0.0 us)
Async XLA Ops:
  0.6 196.0 %copy-start = (f32[512,512]{1,0:T(8,128)S(1)}, f32[512,512]{1,0:T(8,128)}, u32[]{:S(2)}) copy-start(f32[512,512]{1,0:T(8,128)} %refs_9_.1) | copy-start | bytes 3145732
  0.6 196.0 %copy-start.2 = (f32[7,512]{1,0:T(8,128)S(1)}, f32[7,512]{1,0:T(8,128)}, u32[]{:S(2)}) copy-start(f32[7,512]{1,0:T(8,128)} %refs_5_.1) | copy-start | bytes 43012
  0.7 196.0 %copy-start.3 = (s32[1,1024]{1,0:T(1,128)S(1)}, s32[1,1024]{1,0:T(1,128)}, u32[]{:S(2)}) copy-start(s32[1,1024]{1,0:T(1,128)} %refs_1_.1) | copy-start | bytes 12292
  0.7 196.0 %copy-start.4 = (s32[1,1,512]{2,1,0:T(1,128)S(1)}, s32[1,1,512]{2,1,0:T(1,128)}, u32[]{:S(2)}) copy-start(s32[1,1,512]{2,1,0:T(1,128)} %param.15) | copy-start | bytes 6148
  0.7 196.0 %copy-start.5 = (f32[512]{0:T(512)S(1)}, f32[512]{0:T(512)}, u32[]{:S(2)}) copy-start(f32[512]{0:T(512)} %param.16) | copy-start | bytes 6148
  0.7 196.0 %copy-start.6 = (f32[512]{0:T(512)S(1)}, f32[512]{0:T(512)}, u32[]{:S(2)}) copy-start(f32[512]{0:T(512)} %param.18) | copy-start | bytes 6148
  0.7 196.0 %copy-start.7 = (s32[1,64]{1,0:T(1,128)S(1)}, s32[1,64]{1,0:T(1,128)}, u32[]{:S(2)}) copy-start(s32[1,64]{1,0:T(1,128)} %refs_2_.1) | copy-start | bytes 772
  196.7 3.0 %copy-start.1 = (f32[1024,512]{1,0:T(8,128)S(1)}, f32[1024,512]{1,0:T(8,128)}, u32[]{:S(2)}) copy-start(f32[1024,512]{1,0:T(8,128)} %get-tuple-element.126) | copy-start | bytes 6291460

commit v4 on v3

--- a/solution.py
+++ b/solution.py
@@ -10,6 +10,8 @@
 f32, bf16 = jnp.float32, jnp.bfloat16
 NX = 4
 CH = 32
+NB = 128
+CB = 64
 PAD = 8
 GELU_A = 0.7978845608028654
 GELU_B = 0.044715
@@ -363,7 +365,7 @@
         xhat[at, :] = centre * r
         rstd[at, :] = jnp.broadcast_to(r, (rows, 128))
 
-    each(count // CH, lambda i: norm_rows(pl.multiple_of(i * CH + PAD, 8), CH))
+    each(count // NB, lambda i: norm_rows(pl.multiple_of(i * NB + PAD, 8), NB))
     half = taps_ref.shape[0] // 2
     taps = taps_ref[...]
     cgain = cgain_ref[...]
@@ -393,7 +395,7 @@
     loads[3].wait()
 
     def norm_pooled(i):
-        at = pl.ds(pl.multiple_of(i * CH, CH), CH)
+        at = pl.ds(pl.multiple_of(i * NB, NB), NB)
         v = mixed_v[at, :] / wide(plen[at, :])
         centre = v - jnp.sum(v, axis=1, keepdims=True) * inv
         r = lax.rsqrt(jnp.sum(centre * centre, axis=1, keepdims=True) * inv + NORM_EPS)
@@ -401,10 +403,10 @@
         mixed_v[at, :] = v
         xhat2[at, :] = unit
         norm2[at, :] = (unit * mgain).astype(bf16)
-        rstd2[at, :] = jnp.broadcast_to(r, (CH, 128))
+        rstd2[at, :] = jnp.broadcast_to(r, (NB, 128))
         glow[at, :] = gout_v[at, :].astype(bf16)
 
-    each(segs // CH, norm_pooled)
+    each(segs // NB, norm_pooled)
     loads[1].wait()
     loads[2].wait()
 
@@ -478,7 +480,7 @@
     small[...] = jnp.zeros(small.shape, f32)
 
     def norm_back(i):
-        at = pl.ds(pl.multiple_of(i * CH, CH), CH)
+        at = pl.ds(pl.multiple_of(i * NB, NB), NB)
         g, unit = gnorm[at, :], xhat2[at, :]
         prod = g * unit
         small[0:8, :] += fold8(prod)
@@ -488,7 +490,7 @@
         gp = gout_v[at, :] + wide(rstd2[at, :]) * (dx - a - unit * b)
         val_hi[at, :], val_lo[at, :] = split_hi_lo(gp / wide(plen[at, :]))
 
-    each(segs // CH, norm_back)
+    each(segs // NB, norm_back)
     mgain_part = jnp.sum(small[0:8, :], axis=0, keepdims=True)
     gc[pl.ds(PAD, count), :] = mm(pool_t[...], val_hi[0:segs, :]) + mm(pool_t[...], val_lo[0:segs, :])
     for copy in halo(gc, 2):
@@ -496,27 +498,29 @@
 
     core_done(n_hb - 1)
 
+    n_back = count // CB
+
     def back_rows(i):
-        base = pl.multiple_of(i * CH, CH)
-        own = pl.ds(base + PAD, CH)
+        base = pl.multiple_of(i * CB, CB)
+        own = pl.ds(base + PAD, CB)
         here, unit = sid[own, :], xhat[own, :]
-        gl = jnp.zeros((CH, chans), f32)
-        around = gc[pl.ds(base, CH + 2 * PAD), :]
+        gl = jnp.zeros((CB, chans), f32)
+        around = gc[pl.ds(base, CB + 2 * PAD), :]
         for e in range(-half, half + 1):
-            same = wide(ones_where(sid[pl.ds(base + PAD + e, CH), :] == here)) * rows_from(around, PAD + e, CH)
+            same = wide(ones_where(sid[pl.ds(base + PAD + e, CB), :] == here)) * rows_from(around, PAD + e, CB)
             gl = gl + taps[half - e:half - e + 1, :] * same
             gtap_acc[half - e] += fold8(unit * same)
         dx = gl * cgain
         a = jnp.sum(dx, axis=1, keepdims=True) * inv
         b = jnp.sum(dx * unit, axis=1, keepdims=True) * inv
         gs = gc[own, :] + wide(rstd[own, :]) * (dx - a - unit * b)
-        at = pl.ds(base, CH)
+        at = pl.ds(base, CB)
         val_hi[at, :], val_lo[at, :] = split_hi_lo(gs)
 
-    each(n_chunks - 1, back_rows, 1)
+    each(n_back - 1, back_rows, 1)
     for copy in halo(gc, 2):
         copy.wait_recv()
-    each(2, lambda i: back_rows(i * (n_chunks - 1)))
+    each(2, lambda i: back_rows(i * (n_back - 1)))
 
     def sent_all(i):
         p = lax.rem(me + i, n_seq)
@@ -677,9 +681,7 @@
 
     each(n_dp, lambda o: f_recv(o).wait_recv(), 1)
     gwout_ref[...] = jnp.concatenate([fin[1, c] for c in range(n_cols)], axis=1)
-    for c in range(n_cols):
-        piece = jnp.concatenate([fin[0, c], jnp.zeros((64, 128), f32)], axis=0)
-        gwin_ref[c * 128:(c + 1) * 128, :] = jnp.transpose(piece)[:, 0:64]
+    gwin_ref[...] = jnp.concatenate([fin[0, c] for c in range(n_cols)], axis=1)
 
     each(n_seq, lambda i: send_list(i).wait_send(), 1)
 
@@ -703,6 +705,24 @@
             each(n_seq, lambda i: hop_out(i, *hop).wait_send(), 1)
     store_mixed.wait()
     store_rows.wait()
+
+
+def copy_out(*refs):
+    count = len(refs) // 2
+    sems = refs[-1]
+    copies, used = [], 0
+    for src, dst in zip(refs[:count], refs[count:2 * count]):
+        pieces = 4 if src.shape[0] % 128 == 0 and src.shape[1] % 512 == 0 else 1
+        step = src.shape[0] // pieces
+        for k in range(pieces):
+            at = pl.ds(k * step, step)
+            copies.append(pltpu.make_async_copy(
+                src.at[at] if pieces > 1 else src, dst.at[at] if pieces > 1 else dst, sems.at[used]))
+            used += 1
+    for copy in copies:
+        copy.start()
+    for copy in copies:
+        copy.wait()
 
 
 def make_body(n_dp, n_seq):
@@ -749,7 +769,7 @@
             return pl.pallas_call(
                 lambda *refs: kernel(n_dp, n_seq, cap, spare, *refs),
                 out_shape=(
-                    shape((segs, chans), f32), shape((count, chans), f32), shape((chans, share), f32),
+                    shape((segs, chans), f32), shape((count, chans), f32), shape((share, chans), f32),
                     shape((share, chans), f32), shape(conv_kernel.shape, f32), shape((1, chans), f32),
                     shape((1, chans), f32), shape((8, 128), f32),
                 ),
@@ -767,8 +787,15 @@
         outs = call(even, even // 2, 0, "window_even")
         outs = lax.cond(
             outs[7][0, 0] > 0.0, lambda: call(even + even // 2, 0, 1, "window_full")[:7], lambda: outs[:7])
-        mixed, grows, gwin, gwout, gtaps, gcg, gmg = outs
-        return mixed, grows, gwin, gwout, gtaps, gcg[0], gmg[0]
+        mixed, grows, gwin, gwout, gtaps, gcg, gmg = pl.pallas_call(
+            copy_out,
+            out_shape=tuple(shape(value.shape, f32) for value in outs),
+            in_specs=[any_spec] * 7,
+            out_specs=(any_spec,) * 7,
+            scratch_shapes=[D(16)],
+            name="outputs",
+        )(*outs)
+        return mixed, grows, gwin.T, gwout, gtaps, gcg[0], gmg[0]
 
     return body
 

time: 204 us -> 285 us (1.40)
  Pallas kernels: 194 us -> 282 us
  local copies, waits for them, and re-layouts: 7.99 us -> 1.22 us
    pallas_call x0 -> x1, Pallas kernels: none -> 96.5 us  [body(): pl.pallas_call(copy_out, out_shape=tuple((shape(value.shape, f32) for val...]
    pallas_call x1, Pallas kernels: 194 us -> 185 us  [call(): pl.pallas_call(lambda *refs: kernel(n_dp, n_seq, cap, spare, *refs), out_...]
    unnamed x23 -> x14, local copies, waits for them, and re-layouts: 6.8 us -> 0.03 us
where the time goes in v4:
time: 285 us
  Pallas kernels  282 us (99%)
    pallas_call x1, Pallas kernels, call(): pl.pallas_call(lambda *refs: kernel(n_dp, n_seq, cap, spare, *refs), out_...  185 us
    pallas_call x1, Pallas kernels, body(): pl.pallas_call(copy_out, out_shape=tuple((shape(value.shape, f32) for val...  96.5 us

profile of v4, /device:TPU:1, one launch (start us, length us, event | category | flops | bytes accessed | tf_op | source)
XLA Modules:
  0.0 284.7 jit_solution(4109707799875221154)
XLA Ops:
  0.6 0.0 copy-start
  0.6 0.0 copy-start.1
  0.7 0.0 copy-start.2
  0.7 0.0 copy-start.3
  0.7 0.0 copy-start.4
  0.7 0.0 copy-start.5
  0.7 0.0 copy-start.6
  0.7 185.4 %window_even.1 = (f32[512,512]{1,0:T(8,128)}, f32[1024,512]{1,0:T(8,128)}, f32[64,512]{1,0:T(8,128)S(1)}, f32[64,512]{1,0:T(8,128)S(1)}, f32[7,512]{1,0:T(8,128)...) custom-call(f32[1024,512]{1,0:T(8,128)} %refs_0_.1, s32[1,1024]{1,0:T(1,128)} %refs_1_.1, ...), custom_call_target="tpu_custom_call" | custom-call | tf_op jit(solution)/shard_map/window_even/pallas_call | solution.py:769
  186.1 1.2 slice.3
  187.9 0.0 copy-done
  187.9 0.0 copy-done.1
  187.9 0.0 copy-done.2
  187.9 0.0 copy-done.3
  187.9 0.0 copy-done.4
  188.0 0.0 copy-done.5
  188.0 0.0 copy-done.6
  188.0 96.5 %outputs.1 = (f32[512,512]{1,0:T(8,128)}, f32[1024,512]{1,0:T(8,128)}, f32[64,512]{1,0:T(8,128)}, f32[64,512]{1,0:T(8,128)}, f32[7,512]{1,0:T(8,128)}, /*index=5*/f32[1,512]{1,0:T(1,128)}, f32[1,512]{1,0:T(1,128)}) custom-call(f32[512,512]{1,0:T(8,128)} %get-tuple-element.88.refs_0_, f32[1024,512]{1,0:T(8,128)} %get-tuple-element.89.refs_1_, ...), custom_call_target="tpu_custom_call" | custom-call | tf_op jit(solution)/shard_map/outputs/pallas_call | solution.py:790
  (1 shorter events, 0.0 us)
Async XLA Ops:
  0.6 187.3 %copy-start = (f32[512,512]{1,0:T(8,128)S(1)}, f32[512,512]{1,0:T(8,128)}, u32[]{:S(2)}) copy-start(f32[512,512]{1,0:T(8,128)} %refs_9_.1) | copy-start | bytes 3145732
  0.6 187.3 %copy-start.1 = (f32[7,512]{1,0:T(8,128)S(1)}, f32[7,512]{1,0:T(8,128)}, u32[]{:S(2)}) copy-start(f32[7,512]{1,0:T(8,128)} %refs_5_.1) | copy-start | bytes 43012
  0.7 187.3 %copy-start.2 = (s32[1,1024]{1,0:T(1,128)S(1)}, s32[1,1024]{1,0:T(1,128)}, u32[]{:S(2)}) copy-start(s32[1,1024]{1,0:T(1,128)} %refs_1_.1) | copy-start | bytes 12292
  0.7 187.3 %copy-start.3 = (s32[1,1,512]{2,1,0:T(1,128)S(1)}, s32[1,1,512]{2,1,0:T(1,128)}, u32[]{:S(2)}) copy-start(s32[1,1,512]{2,1,0:T(1,128)} %param.15) | copy-start | bytes 6148
  0.7 187.3 %copy-start.4 = (f32[512]{0:T(512)S(1)}, f32[512]{0:T(512)}, u32[]{:S(2)}) copy-start(f32[512]{0:T(512)} %param.16) | copy-start | bytes 6148
  0.7 187.3 %copy-start.5 = (f32[512]{0:T(512)S(1)}, f32[512]{0:T(512)}, u32[]{:S(2)}) copy-start(f32[512]{0:T(512)} %param.18) | copy-start | bytes 6148
  0.7 187.3 %copy-start.6 = (s32[1,64]{1,0:T(1,128)S(1)}, s32[1,64]{1,0:T(1,128)}, u32[]{:S(2)}) copy-start(s32[1,64]{1,0:T(1,128)} %refs_2_.1) | copy-start | bytes 772

commit v5 on v4

--- a/solution.py
+++ b/solution.py
@@ -709,20 +709,8 @@
 
 def copy_out(*refs):
     count = len(refs) // 2
-    sems = refs[-1]
-    copies, used = [], 0
-    for src, dst in zip(refs[:count], refs[count:2 * count]):
-        pieces = 4 if src.shape[0] % 128 == 0 and src.shape[1] % 512 == 0 else 1
-        step = src.shape[0] // pieces
-        for k in range(pieces):
-            at = pl.ds(k * step, step)
-            copies.append(pltpu.make_async_copy(
-                src.at[at] if pieces > 1 else src, dst.at[at] if pieces > 1 else dst, sems.at[used]))
-            used += 1
-    for copy in copies:
-        copy.start()
-    for copy in copies:
-        copy.wait()
+    for src, dst in zip(refs[:count], refs[count:]):
+        dst[...] = src[...]
 
 
 def make_body(n_dp, n_seq):
@@ -787,12 +775,16 @@
         outs = call(even, even // 2, 0, "window_even")
         outs = lax.cond(
             outs[7][0, 0] > 0.0, lambda: call(even + even // 2, 0, 1, "window_full")[:7], lambda: outs[:7])
+        steps = 4
+        specs = tuple(
+            pl.BlockSpec((value.shape[0] // steps, value.shape[1]), lambda i: (i, 0)) if k < 2
+            else pl.BlockSpec(value.shape, lambda i: (0, 0)) for k, value in enumerate(outs))
         mixed, grows, gwin, gwout, gtaps, gcg, gmg = pl.pallas_call(
             copy_out,
             out_shape=tuple(shape(value.shape, f32) for value in outs),
-            in_specs=[any_spec] * 7,
-            out_specs=(any_spec,) * 7,
-            scratch_shapes=[D(16)],
+            grid=(steps,),
+            in_specs=list(specs),
+            out_specs=specs,
             name="outputs",
         )(*outs)
         return mixed, grows, gwin.T, gwout, gtaps, gcg[0], gmg[0]

time: 285 us -> 193 us (0.68)
  Pallas kernels: 282 us -> 190 us
    pallas_call x1, Pallas kernels: 96.5 us -> 4.31 us  [body(): pl.pallas_call(copy_out, out_shape=tuple((shape(value.shape, f32) for val...]
where the time goes in v5:
time: 193 us; the launch traced here: 192 us
  Pallas kernels  190 us (98%)
    pallas_call x1, Pallas kernels, call(): pl.pallas_call(lambda *refs: kernel(n_dp, n_seq, cap, spare, *refs), out_...  185 us
    pallas_call x1, Pallas kernels, body(): pl.pallas_call(copy_out, out_shape=tuple((shape(value.shape, f32) for val...  4.31 us

profile of v5, /device:TPU:1, one launch (start us, length us, event | category | flops | bytes accessed | tf_op | source)
XLA Modules:
  0.0 192.5 jit_solution(247419177102482769)
XLA Ops:
  0.6 0.0 copy-start
  0.6 0.0 copy-start.1
  0.7 0.0 copy-start.2
  0.7 0.0 copy-start.3
  0.7 0.0 copy-start.4
  0.7 0.0 copy-start.5
  0.7 0.0 copy-start.6
  0.7 185.4 %window_even.1 = (f32[512,512]{1,0:T(8,128)}, f32[1024,512]{1,0:T(8,128)}, f32[64,512]{1,0:T(8,128)S(1)}, f32[64,512]{1,0:T(8,128)S(1)}, f32[7,512]{1,0:T(8,128)...) custom-call(f32[1024,512]{1,0:T(8,128)} %refs_0_.1, s32[1,1024]{1,0:T(1,128)} %refs_1_.1, ...), custom_call_target="tpu_custom_call" | custom-call | tf_op jit(solution)/shard_map/window_even/pallas_call | solution.py:757
  186.1 1.2 slice.3
  187.9 0.0 copy-done
  187.9 0.0 copy-done.1
  187.9 0.0 copy-done.2
  187.9 0.0 copy-done.3
  187.9 0.0 copy-done.4
  188.0 0.0 copy-done.5
  188.0 0.0 copy-done.6
  188.0 4.3 %outputs.1 = (f32[512,512]{1,0:T(8,128)}, f32[1024,512]{1,0:T(8,128)}, f32[64,512]{1,0:T(8,128)}, f32[64,512]{1,0:T(8,128)}, f32[7,512]{1,0:T(8,128)}, /*index=5*/f32[1,512]{1,0:T(1,128)}, f32[1,512]{1,0:T(1,128)}) custom-call(f32[512,512]{1,0:T(8,128)} %get-tuple-element.88.refs_0_, f32[1024,512]{1,0:T(8,128)} %get-tuple-element.89.refs_1_, ...), custom_call_target="tpu_custom_call" | custom-call | tf_op jit(solution)/shard_map/outputs/pallas_call | solution.py:782
  (1 shorter events, 0.0 us)
Async XLA Ops:
  0.6 187.3 %copy-start = (f32[512,512]{1,0:T(8,128)S(1)}, f32[512,512]{1,0:T(8,128)}, u32[]{:S(2)}) copy-start(f32[512,512]{1,0:T(8,128)} %refs_9_.1) | copy-start | bytes 3145732
  0.6 187.3 %copy-start.1 = (f32[7,512]{1,0:T(8,128)S(1)}, f32[7,512]{1,0:T(8,128)}, u32[]{:S(2)}) copy-start(f32[7,512]{1,0:T(8,128)} %refs_5_.1) | copy-start | bytes 43012
  0.7 187.3 %copy-start.2 = (s32[1,1024]{1,0:T(1,128)S(1)}, s32[1,1024]{1,0:T(1,128)}, u32[]{:S(2)}) copy-start(s32[1,1024]{1,0:T(1,128)} %refs_1_.1) | copy-start | bytes 12292
  0.7 187.3 %copy-start.3 = (s32[1,1,512]{2,1,0:T(1,128)S(1)}, s32[1,1,512]{2,1,0:T(1,128)}, u32[]{:S(2)}) copy-start(s32[1,1,512]{2,1,0:T(1,128)} %param.15) | copy-start | bytes 6148
  0.7 187.3 %copy-start.4 = (f32[512]{0:T(512)S(1)}, f32[512]{0:T(512)}, u32[]{:S(2)}) copy-start(f32[512]{0:T(512)} %param.16) | copy-start | bytes 6148
  0.7 187.3 %copy-start.5 = (f32[512]{0:T(512)S(1)}, f32[512]{0:T(512)}, u32[]{:S(2)}) copy-start(f32[512]{0:T(512)} %param.18) | copy-start | bytes 6148
  0.7 187.3 %copy-start.6 = (s32[1,64]{1,0:T(1,128)S(1)}, s32[1,64]{1,0:T(1,128)}, u32[]{:S(2)}) copy-start(s32[1,64]{1,0:T(1,128)} %refs_2_.1) | copy-start | bytes 772
